TPU v7x, 256 devices: a whole 4x4x8 slice. The times are simulated.
256 devices in a mesh: lat: 16 (over y, x_hi, core), lon: 16 (over x_lo, z).
Axes of the slice: x: 4 (x_hi: 2, x_lo: 2; x = x_hi * 2 + x_lo), y: 4, z: 8, core: 2. Of those that a mesh axis runs over, the one named last changes fastest.
Arguments:
- adjoint_in: float32 [384, 768, 288], P('lat', 'lon'), may hold values from -6 to 6
- winds: float32 [384, 768, 144], P('lat', 'lon'), may hold values from -0.35 to 0.35
- vert_mix: float32 [72, 72], replicated
- level_weights: float32 [288], replicated, may hold values from 0.02 to 0.3
- snd_weights: bfloat16 [16, 16, 256, 16, 288], P('lat', 'lon'), may hold values from -6 to 6
- snd_columns: int32 [16, 16, 256, 16], P('lat', 'lon'), may hold values from 0 to 1151
- snd_counts: int32 [16, 16, 256], P('lat', 'lon'), may hold values from 8 to 16, as said below
- basis: float32 [384, 768, 256], P('lat', 'lon')
- owner: int32 [256], replicated, may hold values from 0 to 255, each once
Outputs:
- adjoint_out: float32 [384, 768, 288], P('lat', 'lon')
- grad_owned: float32 [256, 1, 4], P(('lat', 'lon'))
Inputs may be any that keep to these rules, and one draw needn't show every extreme that they name: `snd_counts`: some destination device receives exactly 16 live slots from every device.
All inputs are finite; a program needn't handle non-finite values.
Results may differ from a plain program's by a relative error of at most 0.0003.
Values may be sent and summed in bfloat16 or wider, within the bound.
A program may use at most 128 MiB of HBM per device.

v0:
```python
import math

import jax
import jax.numpy as jnp
from jax import lax
from jax.sharding import PartitionSpec as P

diffusion = 0.05


def padded(array, sides, width):
    for axis, dim in sides:
        peers, length = (lax.axis_size(axis), array.shape[dim])
        up = [(i, (i + 1) % peers) for i in range(peers)]
        down = [(j, i) for i, j in up]
        last = lax.slice_in_dim(array, length - width, length, axis=dim)
        leading = lax.slice_in_dim(array, 0, width, axis=dim)
        before = lax.ppermute(last, axis, up)
        after = lax.ppermute(leading, axis, down)
        array = jnp.concatenate([before, array, after], axis=dim)
    return array


def combine(center, east, west, north, south, winds, vert_mix):
    lat_rows, lon_cols, channels = center.shape
    levels = vert_mix.shape[0]
    tracers = channels // levels
    zonal_wind = winds[..., :levels][:, :, None, :]
    merid_wind = winds[..., levels:][:, :, None, :]

    def to_levels(value):
        return value.reshape(lat_rows, lon_cols, tracers, levels)

    middle = to_levels(center)
    advected = middle + (jnp.maximum(zonal_wind, 0.0) + diffusion) * (to_levels(east) - middle)
    advected = advected + (jnp.maximum(-zonal_wind, 0.0) + diffusion) * (to_levels(west) - middle)
    advected = advected + (jnp.maximum(merid_wind, 0.0) + diffusion) * (to_levels(north) - middle)
    advected = advected + (jnp.maximum(-merid_wind, 0.0) + diffusion) * (to_levels(south) - middle)
    vertical = jnp.einsum("abtl,lm->abtm", advected, vert_mix, precision=lax.Precision.HIGHEST)
    return vertical.reshape(lat_rows, lon_cols, channels)


def advance(extended, winds, vert_mix):
    return combine(
        extended[1:-1, 1:-1],
        extended[1:-1, 2:],
        extended[1:-1, :-2],
        extended[2:, 1:-1],
        extended[:-2, 1:-1],
        winds,
        vert_mix,
    )


def fix_poles(extended, depth):
    position = lax.axis_index("lat")
    last_band = lax.axis_size("lat") - 1
    inner = extended.shape[0] - 2 * depth
    low_edge = extended[depth : depth + 1]
    high_edge = extended[depth + inner - 1 : depth + inner]
    low_part = jnp.where(position == 0, low_edge, extended[:depth])
    high_part = jnp.where(position == last_band, high_edge, extended[depth + inner :])
    return jnp.concatenate([low_part, extended[depth : depth + inner], high_part], axis=0)


def body(
    adjoint_in, winds, vert_mix, level_weights, snd_weights, snd_columns, snd_counts, basis, owner
):
    lat_cells, lon_cells, channels = adjoint_in.shape
    levels = vert_mix.shape[0]
    tracers = channels // levels
    bands = lax.axis_size("lat")
    strips = lax.axis_size("lon")
    devices = bands * strips
    slots = snd_weights.shape[3]
    cells = lat_cells * lon_cells
    slot_ids = lax.broadcasted_iota(jnp.int32, (devices, slots), 1)
    live = slot_ids < snd_counts[0, 0][:, None]
    columns = jnp.where(live, snd_columns[0, 0], -1).reshape(bands, strips, slots)
    weights = snd_weights[0, 0].reshape(bands, strips, slots, channels)
    got_weights, got_columns = (
        lax.all_to_all(
            lax.all_to_all(weights, "lat", split_axis=0, concat_axis=0, tiled=True),
            "lon",
            split_axis=1,
            concat_axis=1,
            tiled=True,
        ),
        lax.all_to_all(
            lax.all_to_all(columns, "lat", split_axis=0, concat_axis=0, tiled=True),
            "lon",
            split_axis=1,
            concat_axis=1,
            tiled=True,
        ),
    )
    total_rows = devices * slots
    block_rows = math.gcd(total_rows, 512)
    turns = total_rows // block_rows
    cell_ids = lax.broadcasted_iota(jnp.int32, (1, cells), 1)

    def absorb(total, block):
        block_weights, block_columns = block
        table = (block_columns[:, None] == cell_ids).astype(jnp.bfloat16)
        added = lax.dot_general(
            table, block_weights, (((0,), (0,)), ((), ())), preferred_element_type=jnp.float32
        )
        return (total + added, None)

    injected, _ = lax.scan(
        absorb,
        jnp.zeros((cells, channels), jnp.float32),
        (got_weights.reshape(turns, block_rows, channels), got_columns.reshape(turns, block_rows)),
    )
    state = adjoint_in + injected.reshape(lat_cells, lon_cells, channels)

    def rim_step(current):
        extended = padded(current, (("lat", 0), ("lon", 1)), 1)
        return advance(fix_poles(extended, 1), winds, vert_mix)

    state = rim_step(rim_step(state))
    sens = jnp.sum(
        state.reshape(cells, tracers, levels) * level_weights.reshape(tracers, levels), axis=2
    )
    patterns = basis.shape[2]
    partial_grad = lax.dot_general(
        basis.reshape(cells, patterns),
        sens,
        (((0,), (0,)), ((), ())),
        precision=lax.Precision.HIGHEST,
        preferred_element_type=jnp.float32,
    )
    block_size = patterns // devices
    select = (owner[:, None] == lax.broadcasted_iota(jnp.int32, (1, devices), 1)).astype(
        jnp.float32
    )
    ordered = jnp.einsum(
        "bd,bjt->djt",
        select,
        partial_grad.reshape(devices, block_size, tracers),
        precision=lax.Precision.HIGHEST,
    )
    owned = lax.psum_scatter(ordered, ("lat", "lon"), scatter_dimension=0, tiled=True)
    owned = owned / jnp.sqrt(jnp.float32(cells * devices))
    return (state, owned)


def solution(mesh):
    return jax.shard_map(
        body,
        mesh=mesh,
        in_specs=(
            P("lat", "lon", None),
            P("lat", "lon", None),
            P(),
            P(),
            P("lat", "lon", None, None, None),
            P("lat", "lon", None, None),
            P("lat", "lon", None),
            P("lat", "lon", None),
            P(),
        ),
        out_specs=(P("lat", "lon", None), P(("lat", "lon"), None, None)),
        check_vma=False,
    )
```

profile of v0, /device:TPU:1, one launch (start us, length us, event | category | flops | bytes accessed | tf_op | source)
XLA Modules:
  0.0 369.9 jit_solution(12781261960306346020)
XLA Ops:
  4.3 8.4 %all-to-all-start = ((s32[16,1,256]{2,1,0:T(1,128)}), s32[16,1,256]{2,1,0:T(1,128)S(1)}, u32[]{:S(2)}, u32[]{:S(2)}) async-start(s32[16,1,256]{2,1,0:T(1,128)} %reshape.108), calls=%async_computation | async-start | bytes 32768 | tf_op jit(solution)/shard_map/all_to_all | solution.py:90
  12.7 5.0 %copy.85 = bf16[1,1,256,16,288]{4,3,2,1,0:T(8,128)(2,1)} copy(bf16[1,1,256,16,288]{2,4,3,1,0:T(8,128)(2,1)} %param.15) | data formatting | bytes 4718592 | tf_op args[4]
  17.7 2.3 all-to-all-done
  20.0 4.9 %all-to-all-start.2 = ((bf16[16,16,16,288]{3,2,1,0:T(8,128)(2,1)}), bf16[16,16,16,288]{3,2,1,0:T(8,128)(2,1)}, u32[]{:S(2)}, u32[]{:S(2)}) async-start(bf16[16,16,16,288]{3,2,1,0:T(8,128)(2,1)} %bitcast.37), calls=%async_computation.2 | async-start | bytes 6291456 | tf_op jit(solution)/shard_map/all_to_all | solution.py:83
  27.1 37.7 %all-to-all-done.2 = bf16[16,16,16,288]{3,2,1,0:T(8,128)(2,1)} async-done(((bf16[16,16,16,288]{3,2,1,0:T(8,128)(2,1)}), bf16[16,16,16,288]{3,2,1,0:T(8,128)(2,1)}, u32[]{:S(2)}, u32[]{:S(2)}) %all-to-all-start.2) | async-done | bytes 2359328 | tf_op jit(solution)/shard_map/all_to_all | solution.py:83
  64.8 8.3 %all-to-all-start.1 = ((s32[16,1,256]{2,1,0:T(1,128)}), s32[16,1,256]{2,1,0:T(1,128)S(1)}, u32[]{:S(2)}, u32[]{:S(2)}) async-start(s32[16,1,256]{2,1,0:T(1,128)} %reshape.110), calls=%async_computation.1 | async-start | bytes 32768 | tf_op jit(solution)/shard_map/all_to_all | solution.py:89
  73.1 4.1 %copy.86 = bf16[16,16,16,288]{3,2,0,1:T(8,128)(2,1)} copy(bf16[16,16,16,288]{3,2,1,0:T(8,128)(2,1)} %all-to-all-done.2) | data formatting | bytes 4718592 | tf_op jit(solution)/shard_map/all_to_all | solution.py:83
  77.2 3.3 all-to-all-done.1
  80.5 4.5 %all-to-all-start.3 = ((bf16[16,16,16,288]{3,2,0,1:T(8,128)(2,1)}), bf16[16,16,16,288]{3,2,0,1:T(8,128)(2,1)}, u32[]{:S(2)}, u32[]{:S(2)}) async-start(bf16[16,16,16,288]{3,2,0,1:T(8,128)(2,1)} %copy.86), calls=%async_computation.3 | async-start | bytes 6291456 | tf_op jit(solution)/shard_map/all_to_all | solution.py:82
  85.9 70.4 %all-to-all-done.3 = bf16[16,16,16,288]{3,2,0,1:T(8,128)(2,1)} async-done(((bf16[16,16,16,288]{3,2,0,1:T(8,128)(2,1)}), bf16[16,16,16,288]{3,2,0,1:T(8,128)(2,1)}, u32[]{:S(2)}, u32[]{:S(2)}) %all-to-all-start.3) | async-done | bytes 2359328 | tf_op jit(solution)/shard_map/all_to_all | solution.py:82
  156.3 4.1 %copy.87 = bf16[16,16,16,288]{3,2,1,0:T(8,128)(2,1)} copy(bf16[16,16,16,288]{3,2,0,1:T(8,128)(2,1)} %all-to-all-done.3) | data formatting | bytes 4718592 | tf_op jit(solution)/shard_map/all_to_all | solution.py:82
  160.4 17.1 %while.11 = (s32[]{:T(128)}, f32[1152,288]{0,1:T(8,128)S(1)}, s32[8,512]{1,0:T(8,128)S(1)}, bf16[8,512,288]{2,1,0:T(8,128)(2,1)}, s32[]{:T(128)}, /*index=5*/s32[]{:T(128)}) while((s32[]{:T(128)}, f32[1152,288]{0,1:T(8,128)S(1)}, s32[8,512]{1,0:T(8,128)S(1)}, bf16[8,512,288]{2,1,0:T(8,128)(2,1)}, s32[]{:T(128)}, ...), condition=%wide.region_1.2_spmd.clone, body=%wide.region_0.1_spmd.clone.sunk | while | flops 340992000 | bytes 3054163 | solution.py:110
  179.2 2.2 add.55
  181.5 3.8 %collective-permute-start = (f32[1,48,288]{2,1,0:T(8,128)S(1)}, f32[1,48,288]{2,1,0:T(8,128)S(1)}, u32[]{:S(2)}, u32[]{:S(2)}) collective-permute-start(f32[1,48,288]{2,1,0:T(8,128)S(1)} %get-tuple-element.75), channel_id=1, source_target_pairs={{0,16},{16,32},{32,48},{48,64},{64,80},{80,96},{96,112},{112,128},... | collective-permute-start | bytes 165896 | tf_op jit(solution)/shard_map/ppermute | solution.py:18
  186.7 4.2 %collective-permute-done.1 = f32[1,48,288]{2,1,0:T(8,128)S(1)} collective-permute-done((f32[1,48,288]{2,1,0:T(8,128)S(1)}, f32[1,48,288]{2,1,0:T(8,128)S(1)}, u32[]{:S(2)}, u32[]{:S(2)}) %collective-permute-start.1) | collective-permute-done | bytes 55328 | tf_op jit(solution)/shard_map/ppermute | solution.py:19
  194.2 2.7 reshape.86
  199.4 3.7 %reshape.89 = f32[24,48,4,72]{3,2,1,0:T(4,128)} reshape(f32[24,48,288]{2,1,0:T(8,128)} %get-tuple-element.63) | data formatting | bytes 2654208 | tf_op jit(solution)/shard_map/reshape | solution.py:32
  203.1 3.7 reshape.90
  208.9 3.9 %reshape.87 = f32[24,48,4,72]{3,2,1,0:T(4,128)} reshape(f32[24,48,288]{2,1,0:T(8,128)} %get-tuple-element.71) | data formatting | bytes 2654208 | tf_op jit(solution)/shard_map/reshape | solution.py:32
  212.8 2.7 reshape.88
  215.5 8.0 %fusion.21 = f32[24,48,4,72]{3,1,2,0:T(8,128)S(1)} fusion(f32[24,48,4,72]{3,2,1,0:T(4,128)} %reshape.90, f32[24,48,4,72]{3,2,1,0:T(4,128)} %reshape.89, f32[24,48,4,72]{3,2,1,0:T(4,128)} %reshape.88, f32[24,48,4,72]{3,2,1,0:T(4,128)} %reshape.87, f32[24,48,4,72]{3,2,1,0:T(4,128)} %reshape.86, f32[24,48,72]{2,1,0:T(8,128)} %get-tuple-element.79, ...), kind=kOutput, calls=%fused_computation.24 | convolution fusion | flops 290635776 | bytes 9310464 | tf_op jit(solution)/shard_map/abtl,lm->abtm/dot_general | solution.py:39
  226.8 2.3 copy.99
  229.2 3.4 reshape.91
  246.7 3.9 %collective-permute-done.7 = f32[26,1,288]{2,1,0:T(1,128)} collective-permute-done((f32[26,1,288]{2,1,0:T(1,128)}, f32[26,1,288]{2,1,0:T(1,128)}, u32[]{:S(2)}, u32[]{:S(2)}) %collective-permute-start.7) | collective-permute-done | bytes 29984 | tf_op jit(solution)/shard_map/ppermute | solution.py:18
  250.5 4.2 %pad_maximum_fusion.5 = (f32[24,48,288]{2,1,0:T(8,128)}, f32[24,48,288]{2,1,0:T(8,128)}) fusion(f32[26,1,288]{2,1,0:T(1,128)} %collective-permute-done.6, f32[26,48,288]{2,1,0:T(8,128)} %copy-done.1, f32[26,1,288]{2,1,0:T(1,128)} %collective-permute-done.7), kind=kLoop, calls=%fused_computation.41 | loop fusion | flops 663552 | bytes 4151808 | tf_op jit(solution)/shard_map/concatenate | solution.py:20
  254.7 3.7 reshape.92
  258.4 3.7 reshape.93
  268.2 3.8 %reshape.94 = f32[24,48,4,72]{3,2,1,0:T(4,128)} reshape(f32[24,48,288]{2,1,0:T(8,128)} %get-tuple-element.61) | data formatting | bytes 2654208 | tf_op jit(solution)/shard_map/reshape | solution.py:32
  272.0 3.7 %reshape.95 = f32[24,48,4,72]{3,2,1,0:T(4,128)} reshape(f32[24,48,288]{2,1,0:T(8,128)} %get-tuple-element.62) | data formatting | bytes 2654208 | tf_op jit(solution)/shard_map/reshape | solution.py:32
  275.7 8.5 %multiply_reduce_fusion = (f32[24,48,4]{1,2,0:T(4,128)}, f32[24,48,4,72]{3,1,2,0:T(8,128)S(1)}) fusion(f32[4,72]{1,0:T(4,128)S(1)} %mul.79, f32[72,72]{1,0:T(8,128)} %param.13, f32[24,48,4,72]{3,1,2,0:T(8,128)S(1)} %fusion.21, f32[24,48,4,72]{3,2,1,0:T(4,128)} %reshape.95, f32[24,48,4,72]{3,2,1,0:T(4,128)} %reshape.94, f32[24,48,4,72]{3,2,1,0:T(4,128)} %reshape.93, ...), kind=kOutput, calls=%fused_computation.35 | convolution fusion | flops 291294720 | bytes 9330048 | tf_op jit(solution)/shard_map/abtl,lm->abtm/dot_general | solution.py:39
  285.1 2.4 reshape.96
  289.5 79.9 %all-reduce = f32[256,1,4]{2,1,0:T(1,128)S(1)} all-reduce(f32[256,1,4]{2,1,0:T(1,128)S(1)} %bitcast.44), channel_id=2, replica_groups=mesh['lat'=16,'lon'=16] {'lat','lon'}, use_global_device_ids=true, to_apply=%region_3.4.clone | all-reduce | flops 1024 | bytes 8192
  (88 shorter events, 61.6 us)
Async XLA Ops:
  0.6 286.9 %copy-start = (f32[24,48,256]{2,1,0:T(8,128)S(1)}, f32[24,48,256]{2,1,0:T(8,128)}, u32[]{:S(2)}) copy-start(f32[24,48,256]{2,1,0:T(8,128)} %param.18) | copy-start | bytes 3538948
  4.3 15.7 %all-to-all-start = ((s32[16,1,256]{2,1,0:T(1,128)}), s32[16,1,256]{2,1,0:T(1,128)S(1)}, u32[]{:S(2)}, u32[]{:S(2)}) async-start(s32[16,1,256]{2,1,0:T(1,128)} %reshape.108), calls=%async_computation | async-start | bytes 32768 | tf_op jit(solution)/shard_map/all_to_all | solution.py:90
  20.0 44.8 %all-to-all-start.2 = ((bf16[16,16,16,288]{3,2,1,0:T(8,128)(2,1)}), bf16[16,16,16,288]{3,2,1,0:T(8,128)(2,1)}, u32[]{:S(2)}, u32[]{:S(2)}) async-start(bf16[16,16,16,288]{3,2,1,0:T(8,128)(2,1)} %bitcast.37), calls=%async_computation.2 | async-start | bytes 6291456 | tf_op jit(solution)/shard_map/all_to_all | solution.py:83
  64.8 15.7 %all-to-all-start.1 = ((s32[16,1,256]{2,1,0:T(1,128)}), s32[16,1,256]{2,1,0:T(1,128)S(1)}, u32[]{:S(2)}, u32[]{:S(2)}) async-start(s32[16,1,256]{2,1,0:T(1,128)} %reshape.110), calls=%async_computation.1 | async-start | bytes 32768 | tf_op jit(solution)/shard_map/all_to_all | solution.py:89
  80.5 75.9 %all-to-all-start.3 = ((bf16[16,16,16,288]{3,2,0,1:T(8,128)(2,1)}), bf16[16,16,16,288]{3,2,0,1:T(8,128)(2,1)}, u32[]{:S(2)}, u32[]{:S(2)}) async-start(bf16[16,16,16,288]{3,2,0,1:T(8,128)(2,1)} %copy.86), calls=%async_computation.3 | async-start | bytes 6291456 | tf_op jit(solution)/shard_map/all_to_all | solution.py:82
  181.4 11.0 %copy-start.4 = (f32[24,48,144]{2,1,0:T(8,128)S(1)}, f32[24,48,144]{2,1,0:T(8,128)}, u32[]{:S(2)}) copy-start(f32[24,48,144]{2,1,0:T(8,128)} %param.12) | copy-start | bytes 1990660
  181.5 5.2 %collective-permute-start = (f32[1,48,288]{2,1,0:T(8,128)S(1)}, f32[1,48,288]{2,1,0:T(8,128)S(1)}, u32[]{:S(2)}, u32[]{:S(2)}) collective-permute-start(f32[1,48,288]{2,1,0:T(8,128)S(1)} %get-tuple-element.75), channel_id=1, source_target_pairs={{0,16},{16,32},{32,48},{48,64},{64,80},{80,96},{96,112},{112,128},... | collective-permute-start | bytes 165896 | tf_op jit(solution)/shard_map/ppermute | solution.py:18
  185.3 5.6 %collective-permute-start.1 = (f32[1,48,288]{2,1,0:T(8,128)S(1)}, f32[1,48,288]{2,1,0:T(8,128)S(1)}, u32[]{:S(2)}, u32[]{:S(2)}) collective-permute-start(f32[1,48,288]{2,1,0:T(8,128)S(1)} %get-tuple-element.76), channel_id=1, source_target_pairs={{16,0},{32,16},{48,32},{64,48},{80,64},{96,80},{112,96},{128,112},... | collective-permute-start | bytes 165896 | tf_op jit(solution)/shard_map/ppermute | solution.py:19
  190.9 6.0 %collective-permute-start.2 = (f32[26,1,288]{2,1,0:T(1,128)S(1)}, f32[26,1,288]{2,1,0:T(1,128)S(1)}, u32[]{:S(2)}, u32[]{:S(2)}) collective-permute-start(f32[26,1,288]{2,1,0:T(1,128)S(1)} %get-tuple-element.74), channel_id=1, source_target_pairs={{1,0},{2,1},{3,2},{4,3},{5,4},{6,5},{7,6},{8,7},{9,8},{10,9},{11,1... | collective-permute-start | bytes 89864 | tf_op jit(solution)/shard_map/ppermute | solution.py:19
  191.0 5.9 %collective-permute-start.3 = (f32[26,1,288]{2,1,0:T(1,128)S(1)}, f32[26,1,288]{2,1,0:T(1,128)S(1)}, u32[]{:S(2)}, u32[]{:S(2)}) collective-permute-start(f32[26,1,288]{2,1,0:T(1,128)S(1)} %get-tuple-element.73), channel_id=1, source_target_pairs={{0,1},{1,2},{2,3},{3,4},{4,5},{5,6},{6,7},{7,8},{8,9},{9,10},{10,1... | collective-permute-start | bytes 89864 | tf_op jit(solution)/shard_map/ppermute | solution.py:18
  208.9 3.9 %copy-start.3 = (f32[24,48,288]{2,1,0:T(8,128)S(1)}, f32[24,48,288]{2,1,0:T(8,128)}, u32[]{:S(2)}) copy-start(f32[24,48,288]{2,1,0:T(8,128)} %get-tuple-element.72) | copy-start | bytes 3981316
  226.4 10.4 %collective-permute-start.4 = (f32[1,48,288]{2,1,0:T(8,128)}, f32[1,48,288]{2,1,0:T(8,128)}, u32[]{:S(2)}, u32[]{:S(2)}) collective-permute-start(f32[1,48,288]{2,1,0:T(8,128)} %slice.126), channel_id=1, source_target_pairs={{0,16},{16,32},{32,48},{48,64},{64,80},{80,96},{96,112},{112,128},... | collective-permute-start | bytes 165896 | tf_op jit(solution)/shard_map/ppermute | solution.py:18
  232.5 12.7 %copy-start.5 = (f32[288]{0:T(512)S(1)}, f32[288]{0:T(512)}, u32[]{:S(2)}) copy-start(f32[288]{0:T(512)} %param.14) | copy-start | bytes 3460
  235.8 5.5 %collective-permute-start.5 = (f32[1,48,288]{2,1,0:T(8,128)}, f32[1,48,288]{2,1,0:T(8,128)S(1)}, u32[]{:S(2)}, u32[]{:S(2)}) collective-permute-start(f32[1,48,288]{2,1,0:T(8,128)} %slice.128), channel_id=1, source_target_pairs={{16,0},{32,16},{48,32},{64,48},{80,64},{96,80},{112,96},{128,112},... | collective-permute-start | bytes 165896 | tf_op jit(solution)/shard_map/ppermute | solution.py:19
  241.3 1.3 copy-start.1
  243.3 3.4 collective-permute-start.6
  245.3 5.3 %collective-permute-start.7 = (f32[26,1,288]{2,1,0:T(1,128)}, f32[26,1,288]{2,1,0:T(1,128)}, u32[]{:S(2)}, u32[]{:S(2)}) collective-permute-start(f32[26,1,288]{2,1,0:T(1,128)} %get-tuple-element.69), channel_id=1, source_target_pairs={{0,1},{1,2},{2,3},{3,4},{4,5},{5,6},{6,7},{7,8},{8,9},{9,10},{10,1... | collective-permute-start | bytes 89864 | tf_op jit(solution)/shard_map/ppermute | solution.py:18
  263.9 1.5 copy-start.2
  285.1 3.9 %copy-start.6 = (s32[256]{0:T(256)S(1)}, s32[256]{0:T(256)}, u32[]{:S(2)}) copy-start(s32[256]{0:T(256)} %param.19) | copy-start | bytes 3076
where the time goes:
time: 371 us; the launch traced here: 370 us
  waiting for transfers between devices  126 us (34%)
  blocking collectives  79.9 us (22%)
  local copies, waits for them, and re-layouts  71.8 us (19%)
  matrix products  35.1 us (9%)
  starting transfers between devices  34.9 us (9%)
  other arithmetic  20.5 us (6%)
    unnamed x1, blocking collectives  79.9 us
    all_to_all x1, waiting for transfers between devices, body(): lax.all_to_all(lax.all_to_all(weights, 'lat', split_axis=0, concat_axis=0...  70.4 us
    all_to_all x1, waiting for transfers between devices, body(): lax.all_to_all(weights, 'lat', split_axis=0, concat_axis=0, tiled=True)  37.7 us
    reshape x9, local copies, waits for them, and re-layouts, to_levels(): return value.reshape(lat_rows, lon_cols, tracers, levels)  31.5 us
    dot_general x8, matrix products, absorb(): lax.dot_general(table, block_weights, (((0,), (0,)), ((), ())), preferred...  16.8 us
    dot_general x2, matrix products, combine(): jnp.einsum('abtl,lm->abtm', advected, vert_mix, precision=lax.Precision.H...  16.4 us
    unnamed x22, local copies, waits for them, and re-layouts  12.3 us
    all_to_all x1, starting transfers between devices, body(): lax.all_to_all(columns, 'lat', split_axis=0, concat_axis=0, tiled=True)  8.45 us
  transfers between devices with their start and end apart: 12, of which 9 were waited for; matrix products, arithmetic and copies ran while one was open for 8% of the time, Pallas kernels for 0%

commit v1 on v0

--- a/solution.py
+++ b/solution.py
@@ -1,11 +1,18 @@
+import functools
 import math
 
 import jax
 import jax.numpy as jnp
 from jax import lax
+from jax.experimental import pallas as pl
+from jax.experimental.pallas import tpu as pltpu
 from jax.sharding import PartitionSpec as P
 
 diffusion = 0.05
+MESH = pl.DeviceIdType.MESH
+CELLS = 1152
+CHUNK = 384
+LAG = 3
 
 
 def padded(array, sides, width):
@@ -63,56 +70,185 @@
     return jnp.concatenate([low_part, extended[depth : depth + inner], high_part], axis=0)
 
 
+def offsets(i):
+    j = i - 31
+    a_far, b_far = 1 + j // 15, 1 + j % 15
+    lat_off = jnp.where(i < 16, i, jnp.where(i < 31, 0, a_far))
+    lon_off = jnp.where(i < 16, 0, jnp.where(i < 31, i - 15, b_far))
+    return lat_off, lon_off
+
+
+def target(a, b, lat_off, lon_off):
+    y, x_hi, core = a // 4, (a // 2) % 2, a % 2
+    x_lo, z = b // 8, b % 8
+    zi = lon_off // 2
+    dz = jnp.where(zi % 2 == 1, (zi + 1) // 2, (8 - zi // 2) % 8)
+    y = (y + lat_off // 4) % 4
+    x_hi = (x_hi + (lat_off // 2) % 2) % 2
+    core = (core + lat_off % 2) % 2
+    z = (z + dz) % 8
+    x_lo = (x_lo + lon_off % 2) % 2
+    return (y * 2 + x_hi) * 2 + core, x_lo * 8 + z
+
+
+def exchange_kernel(
+    w, r, k, adj, out, recv, recr, reck, acc, stage, rhs, adj_v, pair_sem, ssem, rsem, lsem
+):
+    a = lax.axis_index("lat")
+    b = lax.axis_index("lon")
+    me = a * 16 + b
+    bar = pltpu.get_barrier_semaphore()
+
+    def greet(i, _):
+        pl.semaphore_signal(bar, inc=1, device_id=((a + i) % 16, b), device_id_type=MESH)
+        pl.semaphore_signal(bar, inc=1, device_id=(a, (b + i) % 16), device_id_type=MESH)
+        return 0
+
+    lax.fori_loop(1, 16, greet, 0)
+    load = pltpu.make_async_copy(adj, adj_v, lsem.at[0])
+    load.start()
+    pltpu.make_async_copy(w.at[me, :, 0:256], recv.at[0], rsem.at[0, 0]).start()
+    pltpu.make_async_copy(r.at[me], recr.at[0], rsem.at[1, 0]).start()
+    pltpu.make_async_copy(k.at[me], reck.at[0], rsem.at[2, 0]).start()
+    acc[...] = jnp.zeros_like(acc)
+    pl.semaphore_wait(bar, 30)
+
+    def ready(i, _):
+        pl.semaphore_signal(pair_sem, inc=1, device_id=(a, (b + i) % 16), device_id_type=MESH)
+        return 0
+
+    lax.fori_loop(1, 16, ready, 0)
+
+    def send(i, _):
+        ta, tb = target(a, b, *offsets(i))
+        d = ta * 16 + tb
+        g = i // 16
+        for n, (src, dst) in enumerate(
+            ((w.at[d, :, 0:256], recv.at[i]), (r.at[d], recr.at[i]), (k.at[d], reck.at[i]))
+        ):
+            pltpu.make_async_remote_copy(
+                src_ref=src,
+                dst_ref=dst,
+                send_sem=ssem.at[n],
+                recv_sem=rsem.at[n, g],
+                device_id=(ta, tb),
+                device_id_type=MESH,
+            ).start()
+        return 0
+
+    lax.fori_loop(1, 31, send, 0)
+    pl.semaphore_wait(pair_sem, 15)
+
+    rows = lax.broadcasted_iota(jnp.int32, (256, 64), 0)
+    cols = lax.broadcasted_iota(jnp.int32, (256, 64), 1)
+    spread = ((rows // 16 == cols // 4) & (rows % 4 == cols % 4)).astype(jnp.bfloat16)
+    rows = lax.broadcasted_iota(jnp.int32, (256, 128), 0)
+    lanes = lax.broadcasted_iota(jnp.int32, (256, 128), 1)
+    keep = ((rows // 4) % 4 == lanes // 32).astype(jnp.float32)
+
+    def absorb(g):
+        first = g * 16
+        for n, buf in enumerate((recv, recr, reck)):
+            part = buf.at[pl.ds(first, 16)]
+            pltpu.make_async_copy(part, part, rsem.at[n, g]).wait()
+        rhs[:, 0:256] = recv[pl.ds(first, 16)].reshape(256, 256)
+        for m in range(16):
+            stage[4 * m : 4 * m + 4, :] = recr[first + m].astype(jnp.float32)
+        packed = stage[...].astype(jnp.bfloat16)
+        wide = jnp.dot(spread, packed, preferred_element_type=jnp.float32) * keep
+        rhs[:, 256:384] = wide.astype(jnp.bfloat16)
+        low = reck[first]
+        high = reck[first + 8]
+        for m in range(1, 8):
+            low = low + reck[first + m]
+            high = high + reck[first + 8 + m]
+        where = jnp.concatenate([low, high], axis=1)
+        for c in range(CELLS // CHUNK):
+            ids = lax.broadcasted_iota(jnp.int32, (CHUNK, 256), 0) + c * CHUNK
+            table = jnp.where(ids == where, 1.0, 0.0).astype(jnp.bfloat16)
+            span = slice(c * CHUNK, (c + 1) * CHUNK)
+            acc[span, :] += jnp.dot(table, rhs[...], preferred_element_type=jnp.float32)
+
+    def turn(c, _):
+        @pl.when(c < 15)
+        def _():
+            lax.fori_loop(31 + c * 15, 46 + c * 15, send, 0)
+
+        @pl.when(c >= LAG)
+        def _():
+            absorb(c - LAG)
+
+        return 0
+
+    lax.fori_loop(0, 16 + LAG, turn, 0)
+    load.wait()
+    out[:, 0:256] = adj_v[:, 0:256] + acc[:, 0:256]
+    tail = acc[:, 256:288] + acc[:, 288:320] + acc[:, 320:352] + acc[:, 352:384]
+    out[:, 256:288] = adj_v[:, 256:288] + tail
+    for n, buf in enumerate((recv, recr, reck)):
+        part = buf.at[pl.ds(1, 255)]
+        pltpu.make_async_copy(part, part, ssem.at[n]).wait()
+
+
+def exchange(adjoint, weights, columns, counts):
+    channels = adjoint.shape[-1]
+    w = weights[0, 0]
+    live = lax.broadcasted_iota(jnp.int32, (256, 16), 1) < counts[0, 0][:, None]
+    where = jnp.where(live, columns[0, 0], -1)
+    r = w[:, :, 256:].reshape(256, 4, 4, 32).transpose(0, 2, 1, 3).reshape(256, 4, 128)
+    a, b = lax.axis_index("lat"), lax.axis_index("lon")
+    dest = lax.broadcasted_iota(jnp.int32, (256, 128), 0)
+    lane = lax.broadcasted_iota(jnp.int32, (256, 128), 1)
+    ta, tb = dest // 16, dest % 16
+    y = (ta // 4 - a // 4 + 4) % 4
+    x_hi = ((ta // 2) % 2 + (a // 2) % 2) % 2
+    core = (ta % 2 + a % 2) % 2
+    lat_off = (y * 2 + x_hi) * 2 + core
+    dz = (tb % 8 - b % 8 + 8) % 8
+    zi = jnp.where(dz == 0, 0, jnp.where(dz <= 4, 2 * dz - 1, 2 * (8 - dz)))
+    lon_off = zi * 2 + (tb // 8 + b // 8) % 2
+    step = jnp.where(
+        lon_off == 0,
+        lat_off,
+        jnp.where(lat_off == 0, 15 + lon_off, 31 + (lat_off - 1) * 15 + lon_off - 1),
+    )
+    spot = jnp.where(step % 8 == lane // 16, jnp.tile(where, (1, 8)), 0)
+    k = spot.reshape(256, 1, 128)
+    return pl.pallas_call(
+        exchange_kernel,
+        out_shape=jax.ShapeDtypeStruct((CELLS, channels), jnp.float32),
+        in_specs=[pl.BlockSpec(memory_space=pl.ANY)] * 4,
+        out_specs=pl.BlockSpec(memory_space=pltpu.VMEM),
+        scratch_shapes=[
+            pltpu.VMEM((256, 16, 256), jnp.bfloat16),
+            pltpu.VMEM((256, 4, 128), jnp.bfloat16),
+            pltpu.VMEM((256, 1, 128), jnp.int32),
+            pltpu.VMEM((CELLS, 384), jnp.float32),
+            pltpu.VMEM((64, 128), jnp.float32),
+            pltpu.VMEM((256, 384), jnp.bfloat16),
+            pltpu.VMEM((CELLS, channels), jnp.float32),
+            pltpu.SemaphoreType.REGULAR,
+            pltpu.SemaphoreType.DMA((3,)),
+            pltpu.SemaphoreType.DMA((3, 16)),
+            pltpu.SemaphoreType.DMA((1,)),
+        ],
+        compiler_params=pltpu.CompilerParams(
+            collective_id=0, has_side_effects=True, vmem_limit_bytes=40 << 20
+        ),
+        name="exchange",
+    )(w, r, k, adjoint.reshape(CELLS, channels))
+
+
 def body(
     adjoint_in, winds, vert_mix, level_weights, snd_weights, snd_columns, snd_counts, basis, owner
 ):
     lat_cells, lon_cells, channels = adjoint_in.shape
     levels = vert_mix.shape[0]
     tracers = channels // levels
-    bands = lax.axis_size("lat")
-    strips = lax.axis_size("lon")
-    devices = bands * strips
-    slots = snd_weights.shape[3]
+    devices = lax.axis_size("lat") * lax.axis_size("lon")
     cells = lat_cells * lon_cells
-    slot_ids = lax.broadcasted_iota(jnp.int32, (devices, slots), 1)
-    live = slot_ids < snd_counts[0, 0][:, None]
-    columns = jnp.where(live, snd_columns[0, 0], -1).reshape(bands, strips, slots)
-    weights = snd_weights[0, 0].reshape(bands, strips, slots, channels)
-    got_weights, got_columns = (
-        lax.all_to_all(
-            lax.all_to_all(weights, "lat", split_axis=0, concat_axis=0, tiled=True),
-            "lon",
-            split_axis=1,
-            concat_axis=1,
-            tiled=True,
-        ),
-        lax.all_to_all(
-            lax.all_to_all(columns, "lat", split_axis=0, concat_axis=0, tiled=True),
-            "lon",
-            split_axis=1,
-            concat_axis=1,
-            tiled=True,
-        ),
-    )
-    total_rows = devices * slots
-    block_rows = math.gcd(total_rows, 512)
-    turns = total_rows // block_rows
-    cell_ids = lax.broadcasted_iota(jnp.int32, (1, cells), 1)
-
-    def absorb(total, block):
-        block_weights, block_columns = block
-        table = (block_columns[:, None] == cell_ids).astype(jnp.bfloat16)
-        added = lax.dot_general(
-            table, block_weights, (((0,), (0,)), ((), ())), preferred_element_type=jnp.float32
-        )
-        return (total + added, None)
-
-    injected, _ = lax.scan(
-        absorb,
-        jnp.zeros((cells, channels), jnp.float32),
-        (got_weights.reshape(turns, block_rows, channels), got_columns.reshape(turns, block_rows)),
-    )
-    state = adjoint_in + injected.reshape(lat_cells, lon_cells, channels)
+    state = exchange(adjoint_in, snd_weights, snd_columns, snd_counts)
+    state = state.reshape(lat_cells, lon_cells, channels)
 
     def rim_step(current):
         extended = padded(current, (("lat", 0), ("lon", 1)), 1)

time: 371 us -> 277 us (0.75)
  waiting for transfers between devices: 126 us -> 13.5 us
  Pallas kernels: 0 us -> 71.7 us
  starting transfers between devices: 34.9 us -> 6.99 us
  matrix products: 35.1 us -> 18.4 us
  local copies, waits for them, and re-layouts: 71.8 us -> 63.6 us
    all_to_all x4 -> x0, waiting for transfers between devices: 114 us -> none  [the longest x1 70.4 us: body(): lax.all_to_all(lax.all_to_all(weights, 'lat', split_axis=0, concat_axis=0...]
    pallas_call x0 -> x1, Pallas kernels: none -> 71.7 us  [exchange(): pl.pallas_call(exchange_kernel, out_shape=jax.ShapeDtypeStruct((CELLS, ch...]
    all_to_all x4 -> x0, starting transfers between devices: 26.2 us -> none  [the longest x1 8.45 us: body(): lax.all_to_all(columns, 'lat', split_axis=0, concat_axis=0, tiled=True)]
    dot_general x8 -> x0, matrix products: 16.8 us -> none  [absorb(): lax.dot_general(table, block_weights, (((0,), (0,)), ((), ())), preferred...]
    all_to_all x5 -> x0, local copies, waits for them, and re-layouts: 8.84 us -> none  [the longest x1 4.07 us: body(): lax.all_to_all(weights, 'lat', split_axis=0, concat_axis=0, tiled=True)]
    select_n x1 -> x2, other arithmetic: 0.02 us -> 7.64 us  [the longest x1 6.83 us: exchange(): spot = jnp.where(step % 8 == lane // 16, jnp.tile(where, (1, 8)), 0)]
    unnamed x22 -> x19, local copies, waits for them, and re-layouts: 12.3 us -> 13.5 us
  transfers between devices with their start and end apart: 12 -> 8, of which waited for: 9 -> 5; matrix products, arithmetic and copies ran while one was open for 8% -> 6% of each run, Pallas kernels for 0% -> 0%
where the time goes in v1:
time: 277 us
  blocking collectives  78.9 us (28%)
  Pallas kernels  71.7 us (26%)
  local copies, waits for them, and re-layouts  63.6 us (23%)
  other arithmetic  22.6 us (8%)
  matrix products  18.4 us (7%)
  waiting for transfers between devices  13.5 us (5%)
  starting transfers between devices  6.99 us (3%)
    unnamed x1, blocking collectives  78.9 us
    pallas_call x1, Pallas kernels, exchange(): pl.pallas_call(exchange_kernel, out_shape=jax.ShapeDtypeStruct((CELLS, ch...  71.7 us
    reshape x9, local copies, waits for them, and re-layouts, to_levels(): return value.reshape(lat_rows, lon_cols, tracers, levels)  31.4 us
    dot_general x2, matrix products, combine(): jnp.einsum('abtl,lm->abtm', advected, vert_mix, precision=lax.Precision.H...  16.4 us
    unnamed x19, local copies, waits for them, and re-layouts  13.5 us
    concatenate x5, other arithmetic, padded(): array = jnp.concatenate([before, array, after], axis=dim)  8.38 us
    ppermute x4, waiting for transfers between devices, padded(): after = lax.ppermute(leading, axis, down)  8.34 us
    select_n x1, other arithmetic, exchange(): spot = jnp.where(step % 8 == lane // 16, jnp.tile(where, (1, 8)), 0)  6.83 us
  transfers between devices with their start and end apart: 8, of which 5 were waited for; matrix products, arithmetic and copies ran while one was open for 6% of the time, Pallas kernels for 0%

profile of v1, /device:TPU:1, one launch (start us, length us, event | category | flops | bytes accessed | tf_op | source)
XLA Modules:
  0.0 276.7 jit_solution(5842394857955568892)
XLA Ops:
  1.7 5.0 %copy.42 = bf16[1,1,256,16,288]{4,3,2,1,0:T(8,128)(2,1)} copy(bf16[1,1,256,16,288]{2,4,3,1,0:T(8,128)(2,1)} %param.13) | data formatting | bytes 4718592 | tf_op args[4]
  9.0 6.8 %compare_select_fusion.14.k = s32[256,1,128]{2,1,0:T(1,128)S(1)} fusion(s32[256,1,128]{2,1,0:T(1,128)S(1)} %copy.44, pred[128]{0:T(512)(128)(4,1)S(1)} %compare_and_fusion, pred[256]{0:T(512)(128)(4,1)S(1)} %get-tuple-element.31, pred[256]{0:T(512)(128)(4,1)S(1)} %get-tuple-element.30, s32[128]{0:T(128)S(1)} %get-tuple-element.34, ...), kind=kLoop, calls=%fused_computation.69 | loop fusion | flops 5275648 | bytes 267924 | tf_op jit(solution)/shard_map/jit(_where)/select_n | solution.py:215
  15.9 1.9 copy-done.1
  19.2 71.7 %exchange.1 = f32[1152,288]{1,0:T(8,128)S(1)} custom-call(bf16[256,16,288]{2,1,0:T(8,128)(2,1)S(1)} %bitcast.37, bf16[256,4,128]{2,1,0:T(4,128)(2,1)S(1)} %copy.45.r, s32[256,1,128]{2,1,0:T(1,128)S(1)} %compare_select_fusion.14.k, f32[1152,288]{1,0:T(8,128)S(1)} %bitcast.38), custom_call_target="tpu_custom_call" | custom-call | tf_op jit(solution)/shard_map/exchange/pallas_call | solution.py:217
  91.0 2.0 collective-permute-start
  94.4 3.9 %collective-permute-done.1 = f32[1,48,288]{2,1,0:T(8,128)S(1)} collective-permute-done((f32[1,48,288]{2,1,0:T(8,128)S(1)}, f32[1,48,288]{2,1,0:T(8,128)S(1)}, u32[]{:S(2)}, u32[]{:S(2)}) %collective-permute-start.1) | collective-permute-done | bytes 55328 | tf_op jit(solution)/shard_map/ppermute | solution.py:26
  99.9 1.7 maximum_add_fusion.3
  101.6 2.7 reshape.770
  104.3 2.1 pad_maximum_fusion.11
  106.4 3.7 %reshape.772 = f32[24,48,4,72]{3,2,1,0:T(4,128)} reshape(f32[24,48,288]{2,1,0:T(8,128)} %get-tuple-element.18) | data formatting | bytes 2654208 | tf_op jit(solution)/shard_map/reshape | solution.py:39
  110.1 3.7 %reshape.773 = f32[24,48,4,72]{3,2,1,0:T(4,128)} reshape(f32[24,48,288]{2,1,0:T(8,128)} %get-tuple-element.19) | data formatting | bytes 2654208 | tf_op jit(solution)/shard_map/reshape | solution.py:39
  115.7 3.7 %reshape.774 = f32[24,48,4,72]{3,2,1,0:T(4,128)} reshape(f32[24,48,288]{2,1,0:T(8,128)} %get-tuple-element.10) | data formatting | bytes 2654208 | tf_op jit(solution)/shard_map/reshape | solution.py:39
  119.4 2.8 reshape.775
  122.2 8.0 %fusion.15 = f32[24,48,4,72]{3,1,2,0:T(8,128)S(1)} fusion(f32[24,48,4,72]{3,2,1,0:T(4,128)} %reshape.775, f32[24,48,4,72]{3,2,1,0:T(4,128)} %reshape.774, f32[24,48,4,72]{3,2,1,0:T(4,128)} %reshape.773, f32[24,48,4,72]{3,2,1,0:T(4,128)} %reshape.772, f32[24,48,4,72]{3,2,1,0:T(4,128)} %reshape.770, f32[24,48,72]{2,1,0:T(8,128)} %get-tuple-element.26, ...), kind=kOutput, calls=%fused_computation.16 | convolution fusion | flops 290635776 | bytes 9310464 | tf_op jit(solution)/shard_map/abtl,lm->abtm/dot_general | solution.py:46
  131.5 1.6 slice.138
  133.1 1.8 collective-permute-start.4
  135.0 2.3 copy.56
  137.3 3.4 %reshape.776 = f32[24,48,288]{2,1,0:T(8,128)} reshape(f32[24,48,4,72]{3,2,1,0:T(4,128)} %copy.56) | data formatting | bytes 2654208 | tf_op jit(solution)/shard_map/reshape | solution.py:47
  142.3 1.6 slice.140
  146.4 3.0 %collective-permute-done.5 = f32[1,48,288]{2,1,0:T(8,128)S(1)} collective-permute-done((f32[1,48,288]{2,1,0:T(8,128)}, f32[1,48,288]{2,1,0:T(8,128)S(1)}, u32[]{:S(2)}, u32[]{:S(2)}) %collective-permute-start.5) | collective-permute-done | bytes 55328 | tf_op jit(solution)/shard_map/ppermute | solution.py:26
  151.4 1.6 collective-permute-start.6
  154.6 3.7 %collective-permute-done.7 = f32[26,1,288]{2,1,0:T(1,128)} collective-permute-done((f32[26,1,288]{2,1,0:T(1,128)}, f32[26,1,288]{2,1,0:T(1,128)}, u32[]{:S(2)}, u32[]{:S(2)}) %collective-permute-start.7) | collective-permute-done | bytes 29984 | tf_op jit(solution)/shard_map/ppermute | solution.py:25
  158.3 4.2 %pad_maximum_fusion.5 = (f32[24,48,288]{2,1,0:T(8,128)}, f32[24,48,288]{2,1,0:T(8,128)}) fusion(f32[26,1,288]{2,1,0:T(1,128)} %collective-permute-done.6, f32[26,48,288]{2,1,0:T(8,128)} %copy-done.3, f32[26,1,288]{2,1,0:T(1,128)} %collective-permute-done.7), kind=kLoop, calls=%fused_computation.33 | loop fusion | flops 663552 | bytes 4151808 | tf_op jit(solution)/shard_map/concatenate | solution.py:27
  162.5 3.7 %reshape.777 = f32[24,48,4,72]{3,2,1,0:T(4,128)} reshape(f32[24,48,288]{2,1,0:T(8,128)} %get-tuple-element.14) | data formatting | bytes 2654208 | tf_op jit(solution)/shard_map/reshape | solution.py:39
  166.2 3.7 %reshape.778 = f32[24,48,4,72]{3,2,1,0:T(4,128)} reshape(f32[24,48,288]{2,1,0:T(8,128)} %get-tuple-element.15) | data formatting | bytes 2654208 | tf_op jit(solution)/shard_map/reshape | solution.py:39
  169.8 1.8 pad_maximum_fusion.1
  173.9 2.0 pad_maximum_fusion.3
  176.0 3.8 %reshape.779 = f32[24,48,4,72]{3,2,1,0:T(4,128)} reshape(f32[24,48,288]{2,1,0:T(8,128)} %get-tuple-element.8) | data formatting | bytes 2654208 | tf_op jit(solution)/shard_map/reshape | solution.py:39
  179.8 3.7 %reshape.780 = f32[24,48,4,72]{3,2,1,0:T(4,128)} reshape(f32[24,48,288]{2,1,0:T(8,128)} %get-tuple-element.9) | data formatting | bytes 2654208 | tf_op jit(solution)/shard_map/reshape | solution.py:39
  183.5 8.5 %multiply_reduce_fusion = (f32[24,48,4]{1,2,0:T(4,128)}, f32[24,48,4,72]{3,1,2,0:T(8,128)S(1)}) fusion(f32[4,72]{1,0:T(4,128)S(1)} %mul.145, f32[72,72]{1,0:T(8,128)} %param.11, f32[24,48,4,72]{3,1,2,0:T(8,128)S(1)} %fusion.15, f32[24,48,4,72]{3,2,1,0:T(4,128)} %reshape.780, f32[24,48,4,72]{3,2,1,0:T(4,128)} %reshape.779, f32[24,48,4,72]{3,2,1,0:T(4,128)} %reshape.778, ...), kind=kOutput, calls=%fused_computation.27 | convolution fusion | flops 291294720 | bytes 9330048 | tf_op jit(solution)/shard_map/abtl,lm->abtm/dot_general | solution.py:46
  192.9 2.4 reshape.781
  197.2 78.9 %all-reduce = f32[256,1,4]{2,1,0:T(1,128)S(1)} all-reduce(f32[256,1,4]{2,1,0:T(1,128)S(1)} %bitcast.42), channel_id=2, replica_groups=mesh['lat'=16,'lon'=16] {'lat','lon'}, use_global_device_ids=true, to_apply=%region_1.2.clone | all-reduce | flops 1024 | bytes 8192
  (57 shorter events, 24.3 us)
Async XLA Ops:
  0.6 194.6 %copy-start = (f32[24,48,256]{2,1,0:T(8,128)S(1)}, f32[24,48,256]{2,1,0:T(8,128)}, u32[]{:S(2)}) copy-start(f32[24,48,256]{2,1,0:T(8,128)} %param.16) | copy-start | bytes 3538948
  15.9 1.9 copy-start.1
  17.8 1.5 copy-start.2
  90.9 8.9 %copy-start.5 = (f32[24,48,144]{2,1,0:T(8,128)S(1)}, f32[24,48,144]{2,1,0:T(8,128)}, u32[]{:S(2)}) copy-start(f32[24,48,144]{2,1,0:T(8,128)} %param.10) | copy-start | bytes 1990660
  91.0 3.4 %collective-permute-start = (f32[1,48,288]{2,1,0:T(8,128)S(1)}, f32[1,48,288]{2,1,0:T(8,128)S(1)}, u32[]{:S(2)}, u32[]{:S(2)}) collective-permute-start(f32[1,48,288]{2,1,0:T(8,128)S(1)} %get-tuple-element.22), channel_id=1, source_target_pairs={{0,16},{16,32},{32,48},{48,64},{64,80},{80,96},{96,112},{112,128},... | collective-permute-start | bytes 165896 | tf_op jit(solution)/shard_map/ppermute | solution.py:25
  93.0 5.3 %collective-permute-start.1 = (f32[1,48,288]{2,1,0:T(8,128)S(1)}, f32[1,48,288]{2,1,0:T(8,128)S(1)}, u32[]{:S(2)}, u32[]{:S(2)}) collective-permute-start(f32[1,48,288]{2,1,0:T(8,128)S(1)} %get-tuple-element.23), channel_id=1, source_target_pairs={{16,0},{32,16},{48,32},{64,48},{80,64},{96,80},{112,96},{128,112},... | collective-permute-start | bytes 165896 | tf_op jit(solution)/shard_map/ppermute | solution.py:26
  98.3 6.0 %collective-permute-start.2 = (f32[26,1,288]{2,1,0:T(1,128)S(1)}, f32[26,1,288]{2,1,0:T(1,128)S(1)}, u32[]{:S(2)}, u32[]{:S(2)}) collective-permute-start(f32[26,1,288]{2,1,0:T(1,128)S(1)} %get-tuple-element.21), channel_id=1, source_target_pairs={{1,0},{2,1},{3,2},{4,3},{5,4},{6,5},{7,6},{8,7},{9,8},{10,9},{11,1... | collective-permute-start | bytes 89864 | tf_op jit(solution)/shard_map/ppermute | solution.py:26
  99.2 5.1 %collective-permute-start.3 = (f32[26,1,288]{2,1,0:T(1,128)S(1)}, f32[26,1,288]{2,1,0:T(1,128)S(1)}, u32[]{:S(2)}, u32[]{:S(2)}) collective-permute-start(f32[26,1,288]{2,1,0:T(1,128)S(1)} %get-tuple-element.20), channel_id=1, source_target_pairs={{0,1},{1,2},{2,3},{3,4},{4,5},{5,6},{6,7},{7,8},{8,9},{9,10},{10,1... | collective-permute-start | bytes 89864 | tf_op jit(solution)/shard_map/ppermute | solution.py:25
  133.1 10.8 %collective-permute-start.4 = (f32[1,48,288]{2,1,0:T(8,128)}, f32[1,48,288]{2,1,0:T(8,128)}, u32[]{:S(2)}, u32[]{:S(2)}) collective-permute-start(f32[1,48,288]{2,1,0:T(8,128)} %slice.138), channel_id=1, source_target_pairs={{0,16},{16,32},{32,48},{48,64},{64,80},{80,96},{96,112},{112,128},... | collective-permute-start | bytes 165896 | tf_op jit(solution)/shard_map/ppermute | solution.py:25
  140.7 12.3 %copy-start.6 = (f32[288]{0:T(512)S(1)}, f32[288]{0:T(512)}, u32[]{:S(2)}) copy-start(f32[288]{0:T(512)} %param.12) | copy-start | bytes 3460
  143.9 5.5 %collective-permute-start.5 = (f32[1,48,288]{2,1,0:T(8,128)}, f32[1,48,288]{2,1,0:T(8,128)S(1)}, u32[]{:S(2)}, u32[]{:S(2)}) collective-permute-start(f32[1,48,288]{2,1,0:T(8,128)} %slice.140), channel_id=1, source_target_pairs={{16,0},{32,16},{48,32},{64,48},{80,64},{96,80},{112,96},{128,112},... | collective-permute-start | bytes 165896 | tf_op jit(solution)/shard_map/ppermute | solution.py:26
  149.4 1.3 copy-start.3
  151.4 3.2 %collective-permute-start.6 = (f32[26,1,288]{2,1,0:T(1,128)}, f32[26,1,288]{2,1,0:T(1,128)}, u32[]{:S(2)}, u32[]{:S(2)}) collective-permute-start(f32[26,1,288]{2,1,0:T(1,128)} %get-tuple-element.17), channel_id=1, source_target_pairs={{1,0},{2,1},{3,2},{4,3},{5,4},{6,5},{7,6},{8,7},{9,8},{10,9},{11,1... | collective-permute-start | bytes 89864 | tf_op jit(solution)/shard_map/ppermute | solution.py:26
  153.0 5.3 %collective-permute-start.7 = (f32[26,1,288]{2,1,0:T(1,128)}, f32[26,1,288]{2,1,0:T(1,128)}, u32[]{:S(2)}, u32[]{:S(2)}) collective-permute-start(f32[26,1,288]{2,1,0:T(1,128)} %get-tuple-element.16), channel_id=1, source_target_pairs={{0,1},{1,2},{2,3},{3,4},{4,5},{5,6},{6,7},{7,8},{8,9},{9,10},{10,1... | collective-permute-start | bytes 89864 | tf_op jit(solution)/shard_map/ppermute | solution.py:25
  171.6 1.5 copy-start.4
  192.9 3.9 %copy-start.7 = (s32[256]{0:T(256)S(1)}, s32[256]{0:T(256)}, u32[]{:S(2)}) copy-start(s32[256]{0:T(256)} %param.17) | copy-start | bytes 3076

commit v2 on v0

v2 whole, which is shorter than its diff:
```python
import jax
import jax.numpy as jnp
from jax import lax
from jax.experimental import pallas as pl
from jax.experimental.pallas import tpu as pltpu
from jax.sharding import PartitionSpec as P

diffusion = 0.05
MESH = pl.DeviceIdType.MESH
BF16 = jnp.bfloat16
F32 = jnp.float32
DEVICES = 256
SIDE = 16
SLOTS = 16
CLAT, CLON = 24, 48
CELLS = CLAT * CLON
CHAN = 288
WIDE = 384
LEV = 72
TRACERS = 4
CHUNK = 384
EAGER = 91
LAG = 2
ROWS = 4


def offsets(i):
    j = i - 31
    lat_off = jnp.where(i < 16, i, jnp.where(i < 31, 0, 1 + j // 15))
    lon_off = jnp.where(i < 16, 0, jnp.where(i < 31, i - 15, 1 + j % 15))
    return lat_off, lon_off


def target(a, b, lat_off, lon_off):
    y, x_hi, core = a // 4, (a // 2) % 2, a % 2
    x_lo, z = b // 8, b % 8
    zi = lon_off // 2
    dz = jnp.where(zi % 2 == 1, (zi + 1) // 2, (8 - zi // 2) % 8)
    y = (y + lat_off // 4) % 4
    x_hi = (x_hi + (lat_off // 2) % 2) % 2
    core = (core + lat_off % 2) % 2
    z = (z + dz) % 8
    x_lo = (x_lo + lon_off % 2) % 2
    return (y * 2 + x_hi) * 2 + core, x_lo * 8 + z


def step_of(a, b, dest):
    ta, tb = dest // 16, dest % 16
    y = (ta // 4 - a // 4 + 4) % 4
    x_hi = ((ta // 2) % 2 + (a // 2) % 2) % 2
    core = (ta % 2 + a % 2) % 2
    lat_off = (y * 2 + x_hi) * 2 + core
    dz = (tb % 8 - b % 8 + 8) % 8
    zi = jnp.where(dz == 0, 0, jnp.where(dz <= 4, 2 * dz - 1, 2 * (8 - dz)))
    lon_off = zi * 2 + (tb // 8 + b // 8) % 2
    far = 31 + (lat_off - 1) * 15 + lon_off - 1
    return jnp.where(lon_off == 0, lat_off, jnp.where(lat_off == 0, 15 + lon_off, far))


def iota(shape, dim):
    return lax.broadcasted_iota(jnp.int32, shape, dim)


def split(value):
    high = value.astype(BF16)
    return high, (value - high.astype(F32)).astype(BF16)


def dot(x, y):
    return jnp.dot(x, y, preferred_element_type=F32)


def window_kernel(
    adj, winds, mix, lweights, w, columns, counts, basis, owner,
    out, grad,
    w_v, f0, f1, fr, wbuf, rbuf, kbuf, recv, recr, reck, acc, stage, rhs,
    adj_v, winds_v, coef, basis_v, base_hi, base_lo, mat, mat_hi, mat_lo,
    cur, nxt, col_out, col_in, mh, ml, sens, part, part_in, total, total_in,
    pair_sem, ssem, rsem, lsem, hs_sem, hr_sem, gs_sem, gr_sem,
):
    a = lax.axis_index("lat")
    b = lax.axis_index("lon")
    me = a * SIDE + b
    bar = pltpu.get_barrier_semaphore()

    def greet(i, _):
        pl.semaphore_signal(bar, inc=1, device_id=((a + i) % SIDE, b), device_id_type=MESH)
        pl.semaphore_signal(bar, inc=1, device_id=(a, (b + i) % SIDE), device_id_type=MESH)
        return 0

    lax.fori_loop(1, SIDE, greet, 0)
    loads = [
        pltpu.make_async_copy(w.at[pl.ds(4 * q, 4)], w_v.at[pl.ds(4 * q, 4)], lsem.at[q])
        for q in range(4)
    ]
    loads.append(pltpu.make_async_copy(adj, adj_v, lsem.at[4]))
    loads.append(pltpu.make_async_copy(winds, winds_v, lsem.at[5]))
    loads.append(pltpu.make_async_copy(basis, basis_v, lsem.at[6]))
    for load in loads:
        load.start()

    slot = iota((SLOTS, DEVICES), 0)
    where = jnp.where(slot < counts[...], columns[...], -1)
    step = step_of(a, b, iota((1, DEVICES), 1))
    placed = jnp.where(iota((128, DEVICES), 0) // SLOTS == step % 8, jnp.concatenate([where] * 8, axis=0), 0)
    for h in range(2):
        kbuf[pl.ds(128 * h, 128), 0, :] = placed[:, 128 * h : 128 * h + 128].T

    for q in range(4):
        loads[q].wait()

        def turn_slot(s, _):
            for h in range(2):
                for c, dst in ((0, f0), (1, f1)):
                    block = w_v[s, 128 * c : 128 * c + 128, 128 * h : 128 * h + 128]
                    dst[pl.ds(2048 * h + s, 128, stride=SLOTS), :] = block.astype(F32).T
            return 0

        lax.fori_loop(4 * q, 4 * q + 4, turn_slot, 0)

    def turn_rest(r, _):
        for h in range(2):
            pieces = [w_v[4 * g + r, 256:288, 128 * h : 128 * h + 128] for g in range(4)]
            block = jnp.concatenate([p.astype(F32) for p in pieces], axis=0)
            fr[pl.ds(512 * h + r, 128, stride=4), :] = block.T
        return 0

    lax.fori_loop(0, 4, turn_rest, 0)

    def pack(d, _):
        n = 8 * d
        rows = pl.ds(pl.multiple_of(SLOTS * n, 128), 128)
        wbuf[pl.ds(n, 8), :, 0:128] = f0[rows, :].astype(BF16).reshape(8, SLOTS, 128)
        wbuf[pl.ds(n, 8), :, 128:256] = f1[rows, :].astype(BF16).reshape(8, SLOTS, 128)
        four = fr[pl.ds(pl.multiple_of(4 * n, 32), 32), :]
        for m in range(8):
            rbuf[n + m] = four[4 * m : 4 * m + 4, :].astype(BF16)
        return 0

    lax.fori_loop(0, DEVICES // 8, pack, 0)

    pl.semaphore_wait(bar, 2 * (SIDE - 1))

    def ready(i, _):
        pl.semaphore_signal(pair_sem, inc=1, device_id=(a, (b + i) % SIDE), device_id_type=MESH)
        return 0

    lax.fori_loop(1, SIDE, ready, 0)

    own = [
        pltpu.make_async_copy(wbuf.at[me], recv.at[0], rsem.at[0, 0]),
        pltpu.make_async_copy(rbuf.at[me], recr.at[0], rsem.at[1, 0]),
        pltpu.make_async_copy(kbuf.at[me], reck.at[0], rsem.at[2, 0]),
    ]
    for copy in own:
        copy.start()

    def send(i, _):
        ta, tb = target(a, b, *offsets(i))
        d = ta * SIDE + tb
        for n, (src, dst) in enumerate(((wbuf, recv), (rbuf, recr), (kbuf, reck))):
            pltpu.make_async_remote_copy(
                src_ref=src.at[d],
                dst_ref=dst.at[i],
                send_sem=ssem.at[n],
                recv_sem=rsem.at[n, i // 16],
                device_id=(ta, tb),
                device_id_type=MESH,
            ).start()
        return 0

    lax.fori_loop(1, 31, send, 0)
    pl.semaphore_wait(pair_sem, SIDE - 1)
    lax.fori_loop(31, EAGER, send, 0)

    mat[...] = jnp.zeros_like(mat)
    for t in range(TRACERS):
        mat[LEV * t : LEV * t + LEV, LEV * t : LEV * t + LEV] = mix[...]
    gain = jnp.sum(mat[:, 0:CHAN] * lweights[...], axis=1, keepdims=True)
    extra = iota((CHAN, WIDE - CHAN), 0) // LEV == iota((CHAN, WIDE - CHAN), 1)
    mat[:, CHAN:WIDE] = jnp.where(extra, gain, 0.0)
    mat_hi[...], mat_lo[...] = split(mat[...])

    loads[6].wait()
    pick = jnp.where(iota((DEVICES, DEVICES), 0) == owner[...], 1.0, 0.0).astype(BF16)
    for c in range(CELLS // 128):
        for piece, dst in zip(split(basis_v[128 * c : 128 * c + 128, :]), (base_hi, base_lo)):
            turned = lax.dot_general(pick, piece, (((1,), (1,)), ((), ())), preferred_element_type=F32)
            dst[:, 128 * c : 128 * c + 128] = turned.astype(BF16)

    loads[4].wait()
    loads[5].wait()
    acc[:, 0:CHAN] = adj_v[...]
    acc[:, CHAN:WIDE] = jnp.zeros((CELLS, WIDE - CHAN), F32)

    def coefficients(r):
        span = pl.ds(pl.multiple_of(r * CLON, CLON), CLON)
        both = winds_v[span, :]
        u = jnp.concatenate([both[:, 0:LEV]] * TRACERS, axis=1)
        v = jnp.concatenate([both[:, LEV : 2 * LEV]] * TRACERS, axis=1)
        east = jnp.maximum(u, 0.0) + diffusion
        west = jnp.maximum(-u, 0.0) + diffusion
        north = jnp.maximum(v, 0.0) + diffusion
        south = jnp.maximum(-v, 0.0) + diffusion
        coef[0, span, :] = 1.0 - ((east + west) + (north + south))
        coef[1, span, :] = east
        coef[2, span, :] = west
        coef[3, span, :] = north
        coef[4, span, :] = south

    rows = iota((DEVICES, 64), 0)
    lanes = iota((DEVICES, 64), 1)
    spread = jnp.where((rows // 16 == lanes // 4) & (rows % 4 == lanes % 4), 1.0, 0.0).astype(BF16)
    rows = iota((DEVICES, 128), 0)
    lanes = iota((DEVICES, 128), 1)
    keep = jnp.where((rows // 4) % 4 == lanes // 32, 1.0, 0.0)

    def absorb(g):
        first = g * 16
        for n, buf in enumerate((recv, recr, reck)):
            piece = buf.at[pl.ds(first, 16)]
            pltpu.make_async_copy(piece, piece, rsem.at[n, g]).wait()
        rhs[:, 0:256] = recv[pl.ds(first, 16)].reshape(256, 256)
        for m in range(16):
            stage[4 * m : 4 * m + 4, :] = recr[first + m].astype(F32)
        rhs[:, 256:384] = (dot(spread, stage[...].astype(BF16)) * keep).astype(BF16)
        low = reck[first]
        high = reck[first + 8]
        for m in range(1, 8):
            low = low + reck[first + m]
            high = high + reck[first + 8 + m]
        spot = jnp.concatenate([low, high], axis=1)
        for c in range(CELLS // CHUNK):
            table = jnp.where(iota((CHUNK, 256), 0) + c * CHUNK == spot, 1.0, 0.0).astype(BF16)
            acc[c * CHUNK : (c + 1) * CHUNK, :] += dot(table, rhs[...])

    chunks = (DEVICES - EAGER) // 15

    def turn(c, _):
        @pl.when(c < chunks)
        def _():
            lax.fori_loop(EAGER + c * 15, EAGER + 15 + c * 15, send, 0)

        @pl.when(c < 12)
        def _():
            coefficients(2 * c)
            coefficients(2 * c + 1)

        @pl.when(c >= LAG)
        def _():
            absorb(c - LAG)

        return 0

    lax.fori_loop(0, 16 + LAG, turn, 0)

    def first_state(r, _):
        span = pl.ds(pl.multiple_of(r * CLON, CLON), CLON)
        row = acc[span, :]
        cur[r + 1, 8:56, 0:256] = row[:, 0:256]
        cur[r + 1, 8:56, 256:288] = (row[:, 256:288] + row[:, 288:320]) + (row[:, 320:352] + row[:, 352:384])
        return 0

    lax.fori_loop(0, CLAT, first_state, 0)

    def copy_to(src, dst, send_sem, recv_sem, ta, tb):
        return pltpu.make_async_remote_copy(
            src_ref=src, dst_ref=dst, send_sem=send_sem, recv_sem=recv_sem, device_id=(ta, tb), device_id_type=MESH
        )

    def halo(buf, e):
        north = copy_to(buf.at[CLAT, 8:56, :], buf.at[0, 8:56, :], hs_sem.at[e, 0], hr_sem.at[e, 0], (a + 1) % SIDE, b)
        south = copy_to(buf.at[1, 8:56, :], buf.at[CLAT + 1, 8:56, :], hs_sem.at[e, 1], hr_sem.at[e, 1], (a + SIDE - 1) % SIDE, b)
        east = copy_to(col_out.at[e, 0], col_in.at[e, 0], hs_sem.at[e, 2], hr_sem.at[e, 2], a, (b + 1) % SIDE)
        west = copy_to(col_out.at[e, 1], col_in.at[e, 1], hs_sem.at[e, 3], hr_sem.at[e, 3], a, (b + SIDE - 1) % SIDE)

        @pl.when(a < SIDE - 1)
        def _():
            north.start()

        @pl.when(a > 0)
        def _():
            south.start()

        col_out[e, 0] = buf[1 : CLAT + 1, 55, :]
        east.start()
        col_out[e, 1] = buf[1 : CLAT + 1, 8, :]
        west.start()

        @pl.when(a > 0)
        def _():
            north.wait_recv()

        @pl.when(a == 0)
        def _():
            buf[0, 8:56, :] = buf[1, 8:56, :]

        @pl.when(a < SIDE - 1)
        def _():
            south.wait_recv()

        @pl.when(a == SIDE - 1)
        def _():
            buf[CLAT + 1, 8:56, :] = buf[CLAT, 8:56, :]

        east.wait_recv()
        buf[1 : CLAT + 1, 7, :] = col_in[e, 0]
        west.wait_recv()
        buf[1 : CLAT + 1, 56, :] = col_in[e, 1]
        return north, south, east, west

    def finish(copies):
        north, south, east, west = copies

        @pl.when(a < SIDE - 1)
        def _():
            north.wait_send()

        @pl.when(a > 0)
        def _():
            south.wait_send()

        east.wait_send()
        west.wait_send()

    def advect(buf, c):
        for k in range(ROWS):
            r = c * ROWS + k
            span = pl.ds(pl.multiple_of(r * CLON, CLON), CLON)
            m = coef[0, span, :] * buf[r + 1, 8:56, 0:CHAN]
            m = m + coef[1, span, :] * buf[r + 1, 9:57, 0:CHAN]
            m = m + coef[2, span, :] * buf[r + 1, 7:55, 0:CHAN]
            m = m + coef[3, span, :] * buf[r + 2, 8:56, 0:CHAN]
            m = m + coef[4, span, :] * buf[r, 8:56, 0:CHAN]
            mh[k * CLON : (k + 1) * CLON, :], ml[k * CLON : (k + 1) * CLON, :] = split(m)

    def step_one(c, _):
        advect(cur, c)
        res = dot(mh[...], mat_hi[:, 0:CHAN]) + dot(ml[...], mat_hi[:, 0:CHAN]) + dot(mh[...], mat_lo[:, 0:CHAN])
        nxt[pl.ds(c * ROWS + 1, ROWS), 8:56, 0:CHAN] = res.reshape(ROWS, CLON, CHAN)
        return 0

    def step_two(c, _):
        advect(nxt, c)
        res = dot(mh[...], mat_hi[...]) + dot(ml[...], mat_hi[...]) + dot(mh[...], mat_lo[...])
        out[pl.ds(c * ROWS, ROWS), :, :] = res[:, 0:CHAN].reshape(ROWS, CLON, CHAN)
        sens[pl.ds(pl.multiple_of(c * ROWS * CLON, ROWS * CLON), ROWS * CLON), :] = res[:, 256:WIDE]
        return 0

    one = halo(cur, 0)
    lax.fori_loop(0, CLAT // ROWS, step_one, 0)
    two = halo(nxt, 1)
    lax.fori_loop(0, CLAT // ROWS, step_two, 0)

    sens_hi, sens_lo = split(sens[...])
    part[...] = dot(base_hi[...], sens_hi) + dot(base_lo[...], sens_hi) + dot(base_hi[...], sens_lo)

    def give_lat(i, _):
        ta = (a + i) % SIDE
        src = part.at[pl.ds(pl.multiple_of(ta * SIDE, SIDE), SIDE)]
        copy_to(src, part_in.at[i], gs_sem.at[0], gr_sem.at[0], ta, b).start()
        return 0

    lax.fori_loop(1, SIDE, give_lat, 0)
    got = part[pl.ds(pl.multiple_of(a * SIDE, SIDE), SIDE), :]
    waiting = part_in.at[pl.ds(1, SIDE - 1)]
    pltpu.make_async_copy(waiting, waiting, gr_sem.at[0]).wait()
    for i in range(1, SIDE):
        got = got + part_in[i]
    total[...] = got

    def give_lon(i, _):
        tb = (b + i) % SIDE
        src = total.at[pl.ds(pl.multiple_of(tb // 8 * 8, 8), 8)]
        copy_to(src, total_in.at[i], gs_sem.at[1], gr_sem.at[1], a, tb).start()
        return 0

    lax.fori_loop(1, SIDE, give_lon, 0)
    mine = total[pl.ds(pl.multiple_of(b // 8 * 8, 8), 8), :]
    landed = total_in.at[pl.ds(1, SIDE - 1)]
    pltpu.make_async_copy(landed, landed, gr_sem.at[1]).wait()
    for i in range(1, SIDE):
        mine = mine + total_in[i]
    row = jnp.sum(jnp.where(iota((8, 128), 0) == b % 8, mine, 0.0), axis=0, keepdims=True)
    scale = 1.0 / jnp.sqrt(jnp.full((1, TRACERS), CELLS * DEVICES, F32))
    grad[...] = row[:, 32 : 32 + TRACERS] * scale

    finish(one)
    finish(two)
    pltpu.make_async_copy(waiting, waiting, gs_sem.at[0]).wait()
    pltpu.make_async_copy(landed, landed, gs_sem.at[1]).wait()
    for n, buf in enumerate((recv, recr, reck)):
        piece = buf.at[pl.ds(1, DEVICES - 1)]
        pltpu.make_async_copy(piece, piece, ssem.at[n]).wait()


def body(
    adjoint_in, winds, vert_mix, level_weights, snd_weights, snd_columns, snd_counts, basis, owner
):
    anywhere = pl.BlockSpec(memory_space=pl.ANY)
    vmem = pl.BlockSpec(memory_space=pltpu.VMEM)
    state, grad = pl.pallas_call(
        window_kernel,
        out_shape=(
            jax.ShapeDtypeStruct((CLAT, CLON, CHAN), F32),
            jax.ShapeDtypeStruct((1, TRACERS), F32),
        ),
        in_specs=[anywhere, anywhere, vmem, vmem, anywhere, vmem, vmem, anywhere, vmem],
        out_specs=(vmem, vmem),
        scratch_shapes=[
            pltpu.VMEM((SLOTS, CHAN, DEVICES), BF16),
            pltpu.VMEM((DEVICES * SLOTS, 128), F32),
            pltpu.VMEM((DEVICES * SLOTS, 128), F32),
            pltpu.VMEM((DEVICES * 4, 128), F32),
            pltpu.VMEM((DEVICES, SLOTS, 256), BF16),
            pltpu.VMEM((DEVICES, 4, 128), BF16),
            pltpu.VMEM((DEVICES, 1, 128), jnp.int32),
            pltpu.VMEM((DEVICES, SLOTS, 256), BF16),
            pltpu.VMEM((DEVICES, 4, 128), BF16),
            pltpu.VMEM((DEVICES, 1, 128), jnp.int32),
            pltpu.VMEM((CELLS, WIDE), F32),
            pltpu.VMEM((64, 128), F32),
            pltpu.VMEM((256, WIDE), BF16),
            pltpu.VMEM((CELLS, CHAN), F32),
            pltpu.VMEM((CELLS, 2 * LEV), F32),
            pltpu.VMEM((5, CELLS, CHAN), F32),
            pltpu.VMEM((CELLS, DEVICES), F32),
            pltpu.VMEM((DEVICES, CELLS), BF16),
            pltpu.VMEM((DEVICES, CELLS), BF16),
            pltpu.VMEM((CHAN, WIDE), F32),
            pltpu.VMEM((CHAN, WIDE), BF16),
            pltpu.VMEM((CHAN, WIDE), BF16),
            pltpu.VMEM((CLAT + 2, 64, WIDE), F32),
            pltpu.VMEM((CLAT + 2, 64, WIDE), F32),
            pltpu.VMEM((2, 2, CLAT, WIDE), F32),
            pltpu.VMEM((2, 2, CLAT, WIDE), F32),
            pltpu.VMEM((ROWS * CLON, CHAN), BF16),
            pltpu.VMEM((ROWS * CLON, CHAN), BF16),
            pltpu.VMEM((CELLS, 128), F32),
            pltpu.VMEM((DEVICES, 128), F32),
            pltpu.VMEM((SIDE, SIDE, 128), F32),
            pltpu.VMEM((SIDE, 128), F32),
            pltpu.VMEM((SIDE, 8, 128), F32),
            pltpu.SemaphoreType.REGULAR,
            pltpu.SemaphoreType.DMA((3,)),
            pltpu.SemaphoreType.DMA((3, 16)),
            pltpu.SemaphoreType.DMA((7,)),
            pltpu.SemaphoreType.DMA((2, 4)),
            pltpu.SemaphoreType.DMA((2, 4)),
            pltpu.SemaphoreType.DMA((2,)),
            pltpu.SemaphoreType.DMA((2,)),
        ],
        compiler_params=pltpu.CompilerParams(
            collective_id=0, has_side_effects=True, vmem_limit_bytes=56 << 20
        ),
        name="window",
    )(
        adjoint_in.reshape(CELLS, CHAN),
        winds.reshape(CELLS, 2 * LEV),
        vert_mix,
        level_weights.reshape(1, CHAN),
        jnp.transpose(snd_weights[0, 0], (1, 2, 0)),
        jnp.transpose(snd_columns[0, 0], (1, 0)),
        snd_counts[0],
        basis.reshape(CELLS, DEVICES),
        owner.reshape(1, DEVICES),
    )
    return state, grad.reshape(1, 1, TRACERS)


def solution(mesh):
    return jax.shard_map(
        body,
        mesh=mesh,
        in_specs=(
            P("lat", "lon", None),
            P("lat", "lon", None),
            P(),
            P(),
            P("lat", "lon", None, None, None),
            P("lat", "lon", None, None),
            P("lat", "lon", None),
            P("lat", "lon", None),
            P(),
        ),
        out_specs=(P("lat", "lon", None), P(("lat", "lon"), None, None)),
        check_vma=False,
    )
```

time: 371 us -> 110 us (0.30)
  waiting for transfers between devices: 126 us -> 0 us
  Pallas kernels: 0 us -> 105 us
  blocking collectives: 79.9 us -> 0 us
  local copies, waits for them, and re-layouts: 71.8 us -> 4.56 us
  matrix products: 35.1 us -> 0 us
  starting transfers between devices: 34.9 us -> 0 us
  other arithmetic: 20.5 us -> 0 us
    all_to_all x4 -> x0, waiting for transfers between devices: 114 us -> none  [the longest x1 70.4 us: body(): lax.all_to_all(lax.all_to_all(weights, 'lat', split_axis=0, concat_axis=0...]
    pallas_call x0 -> x1, Pallas kernels: none -> 105 us  [body(): pl.pallas_call(window_kernel, out_shape=(jax.ShapeDtypeStruct((CLAT, CLON...]
    unnamed x1 -> x0, blocking collectives: 79.9 us -> none
    reshape x12 -> x1, local copies, waits for them, and re-layouts: 37.4 us -> 1.25 us  [body(): level_weights.reshape(1, CHAN)]
    dot_general x12 -> x0, matrix products: 35.1 us -> none  [the longest x8 16.8 us: absorb(): lax.dot_general(table, block_weights, (((0,), (0,)), ((), ())), preferred...]
    all_to_all x4 -> x0, starting transfers between devices: 26.2 us -> none  [the longest x1 8.45 us: body(): lax.all_to_all(columns, 'lat', split_axis=0, concat_axis=0, tiled=True)]
    ppermute x8 -> x0, waiting for transfers between devices: 12.7 us -> none  [the longest x4 7.43 us: padded(): after = lax.ppermute(leading, axis, down)]
    concatenate x7 -> x0, other arithmetic: 12.5 us -> none  [the longest x5 8.43 us: padded(): array = jnp.concatenate([before, array, after], axis=dim)]
  transfers between devices with their start and end apart: 12 -> 0, of which waited for: 9 -> 0; matrix products, arithmetic and copies ran while one was open for 8% -> 0% of each run, Pallas kernels for 0% -> 0%
where the time goes in v2:
time: 110 us
  Pallas kernels  105 us (95%)
  local copies, waits for them, and re-layouts  4.56 us (4%)
    pallas_call x1, Pallas kernels, body(): pl.pallas_call(window_kernel, out_shape=(jax.ShapeDtypeStruct((CLAT, CLON...  105 us
    unnamed x4, local copies, waits for them, and re-layouts  3.31 us

profile of v2, /device:TPU:1, one launch (start us, length us, event | category | flops | bytes accessed | tf_op | source)
XLA Modules:
  0.0 109.7 jit_solution(16290878217688987218)
XLA Ops:
  0.6 1.2 %reshape.24.lweights = f32[1,288]{1,0:T(1,128)} reshape(f32[288]{0:T(512)} %param.12) | data formatting | bytes 2304 | tf_op jit(solution)/shard_map/reshape | solution.py:461
  1.9 104.5 %window.1 = (f32[24,48,288]{2,1,0:T(8,128)}, f32[1,4]{1,0:T(1,128)}) custom-call(f32[1152,288]{1,0:T(8,128)} %bitcast.13, f32[1152,144]{1,0:T(8,128)} %bitcast.14, f32[72,72]{1,0:T(8,128)} %mix.1, f32[1,288]{1,0:T(1,128)} %reshape.24.lweights, bf16[16,288,256]{2,1,0:T(8,128)(2,1)} %bitcast.12, s32[16,256]{1,0:T(8,128)} %bitcast.16, s32[1,256]{1,0:T(1,128)} %bitcast.17, ...), custom_call_target="tpu_custom_call" | custom-call | tf_op jit(solution)/shard_map/window/pallas_call | solution.py:402
  106.4 0.0 copy-start
  106.4 2.8 %copy.13 = f32[24,48,288]{2,1,0:T(8,128)} copy(f32[24,48,288]{2,1,0:T(8,128)} %get-tuple-element.8) | data formatting | bytes 2654208
  109.2 0.0 copy-done
  109.2 0.5 copy.14
Async XLA Ops:
  106.4 2.8 %copy-start = (f32[1,4]{1,0:T(1,128)S(1)}, f32[1,4]{1,0:T(1,128)}, u32[]{:S(2)}) copy-start(f32[1,4]{1,0:T(1,128)} %get-tuple-element.5) | copy-start | bytes 52

commit v3 on v2

v3 whole, which is shorter than its diff:
```python
import jax
import jax.numpy as jnp
from jax import lax
from jax.experimental import pallas as pl
from jax.experimental.pallas import tpu as pltpu
from jax.sharding import PartitionSpec as P

diffusion = 0.05
MESH = pl.DeviceIdType.MESH
BF16 = jnp.bfloat16
F32 = jnp.float32
DEVICES = 256
SIDE = 16
SLOTS = 16
CLAT, CLON = 24, 48
CELLS = CLAT * CLON
CHAN = 288
WIDE = 384
LEV = 72
TRACERS = 4
BAND = 8
LAG = 2
ROWS = 11
RIM = 2 * CLAT + 2 * CLON


def flip(index, by):
    return sum(((index // k) % 2 + (by // k) % 2) % 2 * k for k in (8, 4, 2, 1))


def along(b, lon_off):
    p, f, e = lon_off // 4, (lon_off // 2) % 2, lon_off % 2
    dz = jnp.where(e == 0, p, jnp.where(p == 0, 4, 8 - p))
    return (b // 8 + f) % 2 * 8 + (b % 8 + dz) % 8


def iota(shape, dim):
    return lax.broadcasted_iota(jnp.int32, shape, dim)


def split(value):
    high = value.astype(BF16)
    return high, (value - high.astype(F32)).astype(BF16)


def dot(x, y):
    return jnp.dot(x, y, preferred_element_type=F32)


def window_kernel(
    adj, winds, mix, lweights, w, columns, counts, basis, owner,
    out, grad,
    w_v, f0, f1, fr, wbuf, rbuf, kbuf, kin, kmid, recv, recr, reck, stage, rhs,
    adj_v, winds_v, coef, coef_rim, basis_v, base_hi, base_lo, mat, mat_hi, mat_lo,
    cur, nxt, col_out, col_in, mh, ml, rim, out_v, sens, gsend, gin, grow, gfin,
    pair_sem, ssem, rsem, lsem, ks_sem, kr_sem, hs_sem, hr_sem, gs_sem, gr_sem, out_sem,
):
    a = lax.axis_index("lat")
    b = lax.axis_index("lon")
    me = a * SIDE + b
    bar = pltpu.get_barrier_semaphore()

    def greet(i, _):
        pl.semaphore_signal(bar, inc=1, device_id=((a + i) % SIDE, b), device_id_type=MESH)
        pl.semaphore_signal(bar, inc=1, device_id=(a, (b + i) % SIDE), device_id_type=MESH)
        return 0

    lax.fori_loop(1, SIDE, greet, 0)
    loads = [
        pltpu.make_async_copy(w.at[pl.ds(4 * q, 4)], w_v.at[pl.ds(4 * q, 4)], lsem.at[q])
        for q in range(4)
    ]
    loads.append(pltpu.make_async_copy(adj, adj_v, lsem.at[4]))
    loads.append(pltpu.make_async_copy(winds, winds_v, lsem.at[5]))
    loads.append(pltpu.make_async_copy(basis, basis_v, lsem.at[6]))
    for load in loads:
        load.start()

    def copy_to(src, dst, send_sem, recv_sem, ta, tb):
        return pltpu.make_async_remote_copy(
            src_ref=src, dst_ref=dst, send_sem=send_sem, recv_sem=recv_sem, device_id=(ta, tb), device_id_type=MESH
        )

    slot = iota((SLOTS, DEVICES), 0)
    where = jnp.where(slot < counts[...], columns[...], -1)
    place = flip(a, iota((1, DEVICES), 1) // SIDE) % 8
    placed = jnp.where(iota((128, DEVICES), 0) // SLOTS == place, jnp.concatenate([where] * 8, axis=0), 0)
    for h in range(2):
        kbuf[128 * h : 128 * h + 128, :] = placed[:, 128 * h : 128 * h + 128].T

    def prepare(h, first):
        lanes = pl.ds(pl.multiple_of(128 * h, 128), 128)

        def turn_slot(s, _):
            for c, dst in ((0, f0), (1, f1)):
                block = w_v[s, 128 * c : 128 * c + 128, lanes]
                dst[pl.ds(s, 128, stride=SLOTS), :] = block.astype(F32).T
            return 0

        for q in range(4):
            if first:
                loads[q].wait()
            lax.fori_loop(4 * q, 4 * q + 4, turn_slot, 0)

        def turn_rest(r, _):
            pieces = [w_v[4 * g + r, 256:288, lanes] for g in range(4)]
            block = jnp.concatenate([p.astype(F32) for p in pieces], axis=0)
            fr[pl.ds(r, 128, stride=4), :] = block.T
            return 0

        lax.fori_loop(0, 4, turn_rest, 0)

        def pack(i, _):
            n = 128 * h + 8 * i
            rows = pl.ds(pl.multiple_of(128 * i, 128), 128)
            wbuf[pl.ds(n, 8), :, 0:128] = f0[rows, :].astype(BF16).reshape(8, SLOTS, 128)
            wbuf[pl.ds(n, 8), :, 128:256] = f1[rows, :].astype(BF16).reshape(8, SLOTS, 128)
            four = fr[pl.ds(pl.multiple_of(32 * i, 32), 32), :]
            for m in range(8):
                rbuf[n + m] = four[4 * m : 4 * m + 4, :].astype(BF16)
            return 0

        lax.fori_loop(0, 16, pack, 0)

    def send(lat_off, lon_off):
        ta, tb = flip(a, lat_off), along(b, lon_off)
        d = ta * SIDE + tb
        i = lon_off * SIDE + lat_off
        for n, (src, dst) in enumerate(((wbuf, recv), (rbuf, recr))):
            copy_to(src.at[d], dst.at[i], ssem.at[n], rsem.at[n, lon_off], ta, tb).start()

    def send_lat(lat_off, _):
        send(lat_off, 0)
        return 0

    def send_lon(lon_off, _):
        send(0, lon_off)
        return 0

    prepare(a // 8, True)
    pl.semaphore_wait(bar, 2 * (SIDE - 1))

    def ready(i, _):
        pl.semaphore_signal(pair_sem, inc=1, device_id=(a, (b + i) % SIDE), device_id_type=MESH)
        return 0

    lax.fori_loop(1, SIDE, ready, 0)

    def send_columns(lat_off, _):
        ta = flip(a, lat_off)
        src = kbuf.at[pl.ds(pl.multiple_of(ta * SIDE, SIDE), SIDE)]
        copy_to(src, kin.at[lat_off], ks_sem.at[0], kr_sem.at[0], ta, b).start()
        return 0

    lax.fori_loop(1, SIDE, send_columns, 0)
    lax.fori_loop(1, SIDE, send_lon, 0)
    lax.fori_loop(1, 8, send_lat, 0)
    prepare(1 - a // 8, False)
    lax.fori_loop(8, SIDE, send_lat, 0)
    own = [
        pltpu.make_async_copy(wbuf.at[me], recv.at[0], rsem.at[0, 0]),
        pltpu.make_async_copy(rbuf.at[me], recr.at[0], rsem.at[1, 0]),
    ]
    for copy in own:
        copy.start()

    def pair_of(t):
        return jnp.where(t < 6, t + 2, 7 - t)

    def send_pair(t):
        first = 2 * pair_of(t)

        def both(lat_off, _):
            @pl.when(first > 0)
            def _():
                send(lat_off, first)

            send(lat_off, first + 1)
            return 0

        lax.fori_loop(1, SIDE, both, 0)

    pl.semaphore_wait(pair_sem, SIDE - 1)
    send_pair(0)

    landed = kin.at[pl.ds(1, SIDE - 1)]
    pltpu.make_async_copy(landed, landed, kr_sem.at[0]).wait()
    low = kbuf[pl.ds(pl.multiple_of(a * SIDE, SIDE), SIDE), :]
    high = kin[8]
    for i in range(1, 8):
        low = low + kin[i]
        high = high + kin[8 + i]
    kmid[:, 0, 0:128] = low
    kmid[:, 0, 128:256] = high
    reck[0] = kmid[b]

    def send_rows(lon_off, _):
        tb = along(b, lon_off)
        copy_to(kmid.at[tb], reck.at[lon_off], ks_sem.at[1], kr_sem.at[1], a, tb).start()
        return 0

    lax.fori_loop(1, SIDE, send_rows, 0)
    send_pair(1)

    mat[...] = jnp.zeros_like(mat)
    for t in range(TRACERS):
        mat[LEV * t : LEV * t + LEV, LEV * t : LEV * t + LEV] = mix[...]
    gain = jnp.sum(mat[:, 0:CHAN] * lweights[...].reshape(1, CHAN), axis=1, keepdims=True)
    lane = iota((CHAN, WIDE - CHAN), 1)
    extra = (iota((CHAN, WIDE - CHAN), 0) // LEV == lane % TRACERS) & (lane < TRACERS * SIDE)
    mat[:, CHAN:WIDE] = jnp.where(extra, gain, 0.0)
    mat_hi[...], mat_lo[...] = split(mat[...])

    loads[6].wait()
    pick = jnp.where(iota((DEVICES, DEVICES), 0) == owner[...], 1.0, 0.0).astype(BF16)
    for c in range(CELLS // 128):
        for piece, dst in zip(split(basis_v[128 * c : 128 * c + 128, :]), (base_hi, base_lo)):
            turned = lax.dot_general(pick, piece, (((1,), (1,)), ((), ())), preferred_element_type=F32)
            dst[:, 128 * c : 128 * c + 128] = turned.astype(BF16)

    loads[4].wait()
    loads[5].wait()

    def begin(r, _):
        cur[r + 1, 8:56, 0:CHAN] = adj_v[r]
        cur[r + 1, 8:56, CHAN:WIDE] = jnp.zeros((CLON, WIDE - CHAN), F32)
        return 0

    lax.fori_loop(0, CLAT, begin, 0)

    def coefficients(r):
        both = winds_v[r]
        u = jnp.concatenate([both[:, 0:LEV]] * TRACERS, axis=1)
        v = jnp.concatenate([both[:, LEV : 2 * LEV]] * TRACERS, axis=1)
        east = jnp.maximum(u, 0.0) + diffusion
        west = jnp.maximum(-u, 0.0) + diffusion
        north = jnp.maximum(v, 0.0) + diffusion
        south = jnp.maximum(-v, 0.0) + diffusion
        coef[0, r] = 1.0 - ((east + west) + (north + south))
        coef[1, r] = east
        coef[2, r] = west
        coef[3, r] = north
        coef[4, r] = south

    rows = iota((DEVICES, 64), 0)
    lanes = iota((DEVICES, 64), 1)
    spread = jnp.where((rows // 16 == lanes // 4) & (rows % 4 == lanes % 4), 1.0, 0.0).astype(BF16)
    rows = iota((DEVICES, 128), 0)
    lanes = iota((DEVICES, 128), 1)
    keep = jnp.where((rows // 4) % 4 == lanes // 32, 1.0, 0.0)
    rows = iota((128, 128), 0)
    lanes = iota((128, 128), 1)
    fold = jnp.where(rows % 32 == lanes, 1.0, 0.0).astype(BF16)

    def absorb(g):
        first = g * SIDE
        for n, buf in enumerate((recv, recr)):
            piece = buf.at[pl.ds(first, SIDE)]
            pltpu.make_async_copy(piece, piece, rsem.at[n, g]).wait()
        rhs[:, 0:256] = recv[pl.ds(first, SIDE)].reshape(256, 256)
        for m in range(SIDE):
            stage[4 * m : 4 * m + 4, :] = recr[first + m].astype(F32)
        wide = (dot(spread, stage[...].astype(BF16)) * keep).astype(BF16)
        rhs[:, 256:384] = dot(wide, fold).astype(BF16)
        spot = reck[g]
        for c in range(CLAT // BAND):
            ids = iota((BAND * CLON, 256), 0) + c * BAND * CLON
            table = jnp.where(ids == spot, 1.0, 0.0).astype(BF16)
            cur[c * BAND + 1 : (c + 1) * BAND + 1, 8:56, :] += dot(table, rhs[...]).reshape(BAND, CLON, WIDE)

    coming = reck.at[pl.ds(1, SIDE - 1)]
    pltpu.make_async_copy(coming, coming, kr_sem.at[1]).wait()

    def turn(t, _):
        @pl.when(t < 8)
        def _():
            send_pair(t)

        @pl.when(t < 8)
        def _():
            for i in range(4):
                coefficients(4 * (t - 2) + i)

        first = 2 * pair_of(t - LAG)
        absorb(first)
        absorb(first + 1)
        return 0

    lax.fori_loop(LAG, 8, turn, 0)
    for k in range(5):
        coef_rim[k, 0:CLAT, :] = coef[k, :, 0, :]
        coef_rim[k, CLAT : 2 * CLAT, :] = coef[k, :, CLON - 1, :]

    def last_turns(t, _):
        first = 2 * pair_of(t)
        absorb(first)
        absorb(first + 1)
        return 0

    lax.fori_loop(8 - LAG, 8, last_turns, 0)

    def halo(buf, e):
        north = copy_to(buf.at[CLAT, 8:56, :], buf.at[0, 8:56, :], hs_sem.at[e, 0], hr_sem.at[e, 0], (a + 1) % SIDE, b)
        south = copy_to(buf.at[1, 8:56, :], buf.at[CLAT + 1, 8:56, :], hs_sem.at[e, 1], hr_sem.at[e, 1], (a + SIDE - 1) % SIDE, b)
        east = copy_to(col_out.at[e, 0], col_in.at[e, 0], hs_sem.at[e, 2], hr_sem.at[e, 2], a, (b + 1) % SIDE)
        west = copy_to(col_out.at[e, 1], col_in.at[e, 1], hs_sem.at[e, 3], hr_sem.at[e, 3], a, (b + SIDE - 1) % SIDE)

        @pl.when(a < SIDE - 1)
        def _():
            north.start()

        @pl.when(a > 0)
        def _():
            south.start()

        east.start()
        west.start()
        return north, south, east, west

    def arrive(buf, e, copies):
        north, south, east, west = copies

        @pl.when(a > 0)
        def _():
            north.wait_recv()

        @pl.when(a == 0)
        def _():
            buf[0, 8:56, :] = buf[1, 8:56, :]

        @pl.when(a < SIDE - 1)
        def _():
            south.wait_recv()

        @pl.when(a == SIDE - 1)
        def _():
            buf[CLAT + 1, 8:56, :] = buf[CLAT, 8:56, :]

        east.wait_recv()
        west.wait_recv()

    def finish(copies):
        north, south, east, west = copies

        @pl.when(a < SIDE - 1)
        def _():
            north.wait_send()

        @pl.when(a > 0)
        def _():
            south.wait_send()

        east.wait_send()
        west.wait_send()

    def blend(weights, values):
        m = weights[0] * values[0]
        for k in range(1, 5):
            m = m + weights[k] * values[k]
        return m

    def mixed(high, low, width):
        return dot(high, mat_hi[:, 0:width]) + dot(low, mat_hi[:, 0:width]) + dot(high, mat_lo[:, 0:width])

    def inner(buf, c, width):
        for k in range(ROWS):
            r = 1 + c * ROWS + k
            m = blend(
                [coef[n, r] for n in range(5)],
                [buf[r + 1, 8:56, 0:CHAN], buf[r + 1, 9:57, 0:CHAN], buf[r + 1, 7:55, 0:CHAN],
                 buf[r + 2, 8:56, 0:CHAN], buf[r, 8:56, 0:CHAN]],
            )
            mh[k * CLON : (k + 1) * CLON, :], ml[k * CLON : (k + 1) * CLON, :] = split(m)
        return mixed(mh[...], ml[...], width)

    def outer(buf, e, width):
        west = col_in[e, 0, :, 0:CHAN]
        east = col_in[e, 1, :, 0:CHAN]
        for n, (x, x_west, x_east) in enumerate(((8, west, None), (55, None, east))):
            span = slice(n * CLAT, (n + 1) * CLAT)
            x_west = buf[1 : CLAT + 1, x - 1, 0:CHAN] if x_west is None else x_west
            x_east = buf[1 : CLAT + 1, x + 1, 0:CHAN] if x_east is None else x_east
            rim[span, :] = blend(
                [coef_rim[k, span, :] for k in range(5)],
                [buf[1 : CLAT + 1, x, 0:CHAN], x_east, x_west, buf[2 : CLAT + 2, x, 0:CHAN], buf[0:CLAT, x, 0:CHAN]],
            )
        for n, r in enumerate((0, CLAT - 1)):
            buf[r + 1, 7:8, 0:CHAN] = west[r : r + 1, :]
            buf[r + 1, 56:57, 0:CHAN] = east[r : r + 1, :]
            m = blend(
                [coef[k, r] for k in range(5)],
                [buf[r + 1, 8:56, 0:CHAN], buf[r + 1, 9:57, 0:CHAN], buf[r + 1, 7:55, 0:CHAN],
                 buf[r + 2, 8:56, 0:CHAN], buf[r, 8:56, 0:CHAN]],
            )
            rim[2 * CLAT + n * CLON : 2 * CLAT + (n + 1) * CLON, :] = m
        return mixed(*split(rim[...]), width)

    col_out[0, 0, :, 0:CHAN] = cur[1 : CLAT + 1, 55, 0:CHAN]
    col_out[0, 1, :, 0:CHAN] = cur[1 : CLAT + 1, 8, 0:CHAN]
    one = halo(cur, 0)

    def inner_one(c, _):
        res = inner(cur, c, CHAN).reshape(ROWS, CLON, CHAN)
        nxt[pl.ds(c * ROWS + 2, ROWS), 8:56, 0:CHAN] = res
        return 0

    lax.fori_loop(0, 2, inner_one, 0)
    arrive(cur, 0, one)
    res = outer(cur, 0, CHAN)
    nxt[1 : CLAT + 1, 8, 0:CHAN] = res[0:CLAT]
    nxt[1 : CLAT + 1, 55, 0:CHAN] = res[CLAT : 2 * CLAT]
    nxt[1, 8:56, 0:CHAN] = res[2 * CLAT : 2 * CLAT + CLON]
    nxt[CLAT, 8:56, 0:CHAN] = res[2 * CLAT + CLON : RIM]
    col_out[1, 0, :, 0:CHAN] = res[CLAT : 2 * CLAT]
    col_out[1, 1, :, 0:CHAN] = res[0:CLAT]
    two = halo(nxt, 1)

    def inner_two(c, _):
        res = inner(nxt, c, WIDE)
        out_v[pl.ds(c * ROWS + 1, ROWS)] = res[:, 0:CHAN].reshape(ROWS, CLON, CHAN)
        sens[pl.ds(c * ROWS + 1, ROWS)] = res[:, 256:WIDE].reshape(ROWS, CLON, 128)
        return 0

    lax.fori_loop(0, 2, inner_two, 0)
    arrive(nxt, 1, two)
    res = outer(nxt, 1, WIDE)
    for dst, lanes in ((out_v, slice(0, CHAN)), (sens, slice(256, WIDE))):
        dst[:, 0, :] = res[0:CLAT, lanes]
        dst[:, CLON - 1, :] = res[CLAT : 2 * CLAT, lanes]
        dst[0] = res[2 * CLAT : 2 * CLAT + CLON, lanes]
        dst[CLAT - 1] = res[2 * CLAT + CLON : RIM, lanes]
    leave = pltpu.make_async_copy(out_v, out, out_sem.at[0])
    leave.start()

    sens_hi, sens_lo = split(sens[...].reshape(CELLS, 128))
    part = dot(base_hi[...], sens_hi) + dot(base_lo[...], sens_hi) + dot(base_hi[...], sens_lo)
    rows = iota((DEVICES, 128), 0)
    lanes = iota((DEVICES, 128), 1)
    part = jnp.where((lanes // TRACERS == rows % SIDE + 8) & (lanes >= 32), part, 0.0)
    gsend[:, 0, :] = jnp.sum(part.reshape(SIDE, SIDE, 128), axis=1)

    def give_lat(i, _):
        ta = (a + i) % SIDE
        copy_to(gsend.at[ta], gin.at[i], gs_sem.at[0], gr_sem.at[0], ta, b).start()
        return 0

    lax.fori_loop(1, SIDE, give_lat, 0)
    got = gsend[a]
    lat_in = gin.at[pl.ds(1, SIDE - 1)]
    pltpu.make_async_copy(lat_in, lat_in, gr_sem.at[0]).wait()
    for i in range(1, SIDE):
        got = got + gin[i]
    grow[...] = got

    def give_lon(i, _):
        copy_to(grow, gfin.at[i], gs_sem.at[1], gr_sem.at[1], a, (b + i) % SIDE).start()
        return 0

    lax.fori_loop(1, SIDE, give_lon, 0)
    lon_in = gfin.at[pl.ds(1, SIDE - 1)]
    pltpu.make_async_copy(lon_in, lon_in, gr_sem.at[1]).wait()
    for i in range(1, SIDE):
        got = got + gfin[i]
    lanes = iota((1, 128), 1)
    owned = jnp.zeros((1, TRACERS), F32)
    for t in range(TRACERS):
        value = jnp.sum(jnp.where(lanes == 32 + TRACERS * b + t, got, 0.0), axis=1, keepdims=True)
        owned = jnp.where(iota((1, TRACERS), 1) == t, value, owned)
    grad[...] = owned * (1.0 / jnp.sqrt(jnp.full((1, TRACERS), CELLS * DEVICES, F32)))

    finish(one)
    finish(two)
    leave.wait()
    for piece, sem in ((landed, ks_sem.at[0]), (coming, ks_sem.at[1]), (lat_in, gs_sem.at[0]), (lon_in, gs_sem.at[1])):
        pltpu.make_async_copy(piece, piece, sem).wait()
    for n, buf in enumerate((recv, recr)):
        piece = buf.at[pl.ds(1, DEVICES - 1)]
        pltpu.make_async_copy(piece, piece, ssem.at[n]).wait()


def body(
    adjoint_in, winds, vert_mix, level_weights, snd_weights, snd_columns, snd_counts, basis, owner
):
    anywhere = pl.BlockSpec(memory_space=pl.ANY)
    vmem = pl.BlockSpec(memory_space=pltpu.VMEM)
    state, grad = pl.pallas_call(
        window_kernel,
        out_shape=(
            jax.ShapeDtypeStruct((CLAT, CLON, CHAN), F32),
            jax.ShapeDtypeStruct((1, TRACERS), F32),
        ),
        in_specs=[anywhere, anywhere, vmem, vmem, anywhere, vmem, vmem, anywhere, vmem],
        out_specs=(anywhere, vmem),
        scratch_shapes=[
            pltpu.VMEM((SLOTS, CHAN, DEVICES), BF16),
            pltpu.VMEM((128 * SLOTS, 128), F32),
            pltpu.VMEM((128 * SLOTS, 128), F32),
            pltpu.VMEM((128 * 4, 128), F32),
            pltpu.VMEM((DEVICES, SLOTS, 256), BF16),
            pltpu.VMEM((DEVICES, 4, 128), BF16),
            pltpu.VMEM((DEVICES, 128), jnp.int32),
            pltpu.VMEM((SIDE, SIDE, 128), jnp.int32),
            pltpu.VMEM((SIDE, 1, 256), jnp.int32),
            pltpu.VMEM((DEVICES, SLOTS, 256), BF16),
            pltpu.VMEM((DEVICES, 4, 128), BF16),
            pltpu.VMEM((SIDE, 1, 256), jnp.int32),
            pltpu.VMEM((64, 128), F32),
            pltpu.VMEM((256, WIDE), BF16),
            pltpu.VMEM((CLAT, CLON, CHAN), F32),
            pltpu.VMEM((CLAT, CLON, 2 * LEV), F32),
            pltpu.VMEM((5, CLAT, CLON, CHAN), F32),
            pltpu.VMEM((5, 2 * CLAT, CHAN), F32),
            pltpu.VMEM((CELLS, DEVICES), F32),
            pltpu.VMEM((DEVICES, CELLS), BF16),
            pltpu.VMEM((DEVICES, CELLS), BF16),
            pltpu.VMEM((CHAN, WIDE), F32),
            pltpu.VMEM((CHAN, WIDE), BF16),
            pltpu.VMEM((CHAN, WIDE), BF16),
            pltpu.VMEM((CLAT + 2, 64, WIDE), F32),
            pltpu.VMEM((CLAT + 2, 64, WIDE), F32),
            pltpu.VMEM((2, 2, CLAT, WIDE), F32),
            pltpu.VMEM((2, 2, CLAT, WIDE), F32),
            pltpu.VMEM((ROWS * CLON, CHAN), BF16),
            pltpu.VMEM((ROWS * CLON, CHAN), BF16),
            pltpu.VMEM((RIM, CHAN), F32),
            pltpu.VMEM((CLAT, CLON, CHAN), F32),
            pltpu.VMEM((CLAT, CLON, 128), F32),
            pltpu.VMEM((SIDE, 1, 128), F32),
            pltpu.VMEM((SIDE, 1, 128), F32),
            pltpu.VMEM((1, 128), F32),
            pltpu.VMEM((SIDE, 1, 128), F32),
            pltpu.SemaphoreType.REGULAR,
            pltpu.SemaphoreType.DMA((2,)),
            pltpu.SemaphoreType.DMA((2, SIDE)),
            pltpu.SemaphoreType.DMA((7,)),
            pltpu.SemaphoreType.DMA((2,)),
            pltpu.SemaphoreType.DMA((2,)),
            pltpu.SemaphoreType.DMA((2, 4)),
            pltpu.SemaphoreType.DMA((2, 4)),
            pltpu.SemaphoreType.DMA((2,)),
            pltpu.SemaphoreType.DMA((2,)),
            pltpu.SemaphoreType.DMA((1,)),
        ],
        compiler_params=pltpu.CompilerParams(
            collective_id=0, has_side_effects=True, vmem_limit_bytes=56 << 20
        ),
        name="window",
    )(
        adjoint_in,
        winds,
        vert_mix,
        level_weights,
        jnp.transpose(snd_weights[0, 0], (1, 2, 0)),
        jnp.transpose(snd_columns[0, 0], (1, 0)),
        snd_counts[0],
        basis.reshape(CELLS, DEVICES),
        owner.reshape(1, DEVICES),
    )
    return state, grad.reshape(1, 1, TRACERS)


def solution(mesh):
    return jax.shard_map(
        body,
        mesh=mesh,
        in_specs=(
            P("lat", "lon", None),
            P("lat", "lon", None),
            P(),
            P(),
            P("lat", "lon", None, None, None),
            P("lat", "lon", None, None),
            P("lat", "lon", None),
            P("lat", "lon", None),
            P(),
        ),
        out_specs=(P("lat", "lon", None), P(("lat", "lon"), None, None)),
        check_vma=False,
    )
```

time: 110 us -> 97.9 us (0.89)
  Pallas kernels: 105 us -> 93.7 us
  local copies, waits for them, and re-layouts: 4.56 us -> 3.31 us
    pallas_call x1, Pallas kernels: 105 us -> 93.7 us  [body(): pl.pallas_call(window_kernel, out_shape=(jax.ShapeDtypeStruct((CLAT, CLON...]
    reshape x1 -> x0, local copies, waits for them, and re-layouts: 1.25 us -> none  [body(): level_weights.reshape(1, CHAN)]
where the time goes in v3:
time: 97.9 us; the launch traced here: 97.7 us
  Pallas kernels  93.7 us (96%)
  local copies, waits for them, and re-layouts  3.31 us (3%)
    pallas_call x1, Pallas kernels, body(): pl.pallas_call(window_kernel, out_shape=(jax.ShapeDtypeStruct((CLAT, CLON...  93.7 us
    unnamed x4, local copies, waits for them, and re-layouts  3.31 us

profile of v3, /device:TPU:1, one launch (start us, length us, event | category | flops | bytes accessed | tf_op | source)
XLA Modules:
  0.0 97.7 jit_solution(11525744789621000448)
XLA Ops:
  0.6 93.7 %window.1 = (f32[24,48,288]{2,1,0:T(8,128)}, f32[1,4]{1,0:T(1,128)}) custom-call(f32[24,48,288]{2,1,0:T(8,128)} %adj.1, f32[24,48,144]{2,1,0:T(8,128)} %winds.1, f32[72,72]{1,0:T(8,128)} %mix.1, f32[288]{0:T(512)} %lweights.1, bf16[16,288,256]{2,1,0:T(8,128)(2,1)} %bitcast.10, s32[16,256]{1,0:T(8,128)} %bitcast.12, s32[1,256]{1,0:T(1,128)} %bitcast.13, ...), custom_call_target="tpu_custom_call" | custom-call | tf_op jit(solution)/shard_map/window/pallas_call | solution.py:486
  94.4 0.0 copy-start
  94.4 2.8 %copy.13 = f32[24,48,288]{2,1,0:T(8,128)} copy(f32[24,48,288]{2,1,0:T(8,128)} %get-tuple-element.8) | data formatting | bytes 2654208
  97.2 0.0 copy-done
  97.2 0.5 copy.14
Async XLA Ops:
  94.4 2.8 %copy-start = (f32[1,4]{1,0:T(1,128)S(1)}, f32[1,4]{1,0:T(1,128)}, u32[]{:S(2)}) copy-start(f32[1,4]{1,0:T(1,128)} %get-tuple-element.5) | copy-start | bytes 52

commit v4 on v3

--- a/solution.py
+++ b/solution.py
@@ -30,7 +30,8 @@
 
 def along(b, lon_off):
     p, f, e = lon_off // 4, (lon_off // 2) % 2, lon_off % 2
-    dz = jnp.where(e == 0, p, jnp.where(p == 0, 4, 8 - p))
+    dz = jnp.where(p == 0, 4 * f, jnp.where(e == 0, p, 8 - p))
+    f = jnp.where(p == 0, e, f)
     return (b // 8 + f) % 2 * 8 + (b % 8 + dz) % 8
 
 
@@ -52,7 +53,7 @@
     out, grad,
     w_v, f0, f1, fr, wbuf, rbuf, kbuf, kin, kmid, recv, recr, reck, stage, rhs,
     adj_v, winds_v, coef, coef_rim, basis_v, base_hi, base_lo, mat, mat_hi, mat_lo,
-    cur, nxt, col_out, col_in, mh, ml, rim, out_v, sens, gsend, gin, grow, gfin,
+    cur, nxt, col_out, col_in, row_in, mh, ml, rim, out_v, sens, gsend, gin, grow, gfin,
     pair_sem, ssem, rsem, lsem, ks_sem, kr_sem, hs_sem, hr_sem, gs_sem, gr_sem, out_sem,
 ):
     a = lax.axis_index("lat")
@@ -65,15 +66,20 @@
         pl.semaphore_signal(bar, inc=1, device_id=(a, (b + i) % SIDE), device_id_type=MESH)
         return 0
 
+    halves = [a // 8, 1 - a // 8]
+    loads = []
+    for n, h in enumerate(halves):
+        lanes = pl.ds(pl.multiple_of(128 * h, 128), 128)
+        for q in range(2):
+            eight = pl.ds(8 * q, 8)
+            loads.append(pltpu.make_async_copy(w.at[eight, :, lanes], w_v.at[n, eight], lsem.at[2 * n + q]))
+    for load in loads:
+        load.start()
     lax.fori_loop(1, SIDE, greet, 0)
-    loads = [
-        pltpu.make_async_copy(w.at[pl.ds(4 * q, 4)], w_v.at[pl.ds(4 * q, 4)], lsem.at[q])
-        for q in range(4)
-    ]
     loads.append(pltpu.make_async_copy(adj, adj_v, lsem.at[4]))
     loads.append(pltpu.make_async_copy(winds, winds_v, lsem.at[5]))
     loads.append(pltpu.make_async_copy(basis, basis_v, lsem.at[6]))
-    for load in loads:
+    for load in loads[4:]:
         load.start()
 
     def copy_to(src, dst, send_sem, recv_sem, ta, tb):
@@ -88,39 +94,29 @@
     for h in range(2):
         kbuf[128 * h : 128 * h + 128, :] = placed[:, 128 * h : 128 * h + 128].T
 
-    def prepare(h, first):
-        lanes = pl.ds(pl.multiple_of(128 * h, 128), 128)
-
-        def turn_slot(s, _):
-            for c, dst in ((0, f0), (1, f1)):
-                block = w_v[s, 128 * c : 128 * c + 128, lanes]
-                dst[pl.ds(s, 128, stride=SLOTS), :] = block.astype(F32).T
-            return 0
-
-        for q in range(4):
-            if first:
-                loads[q].wait()
-            lax.fori_loop(4 * q, 4 * q + 4, turn_slot, 0)
-
-        def turn_rest(r, _):
-            pieces = [w_v[4 * g + r, 256:288, lanes] for g in range(4)]
+    def prepare(n):
+        h = halves[n]
+        for q in range(2):
+            loads[2 * n + q].wait()
+            for s in range(8 * q, 8 * q + 8):
+                for c, dst in ((0, f0), (1, f1)):
+                    block = w_v[n, s, 128 * c : 128 * c + 128, :]
+                    dst[pl.ds(s, 128, stride=SLOTS), :] = block.astype(F32).T
+        for r in range(4):
+            pieces = [w_v[n, 4 * g + r, 256:288, :] for g in range(4)]
             block = jnp.concatenate([p.astype(F32) for p in pieces], axis=0)
             fr[pl.ds(r, 128, stride=4), :] = block.T
+
+        def pack(i, _):
+            first = 128 * h + 8 * i
+            rows = pl.ds(pl.multiple_of(128 * i, 128), 128)
+            wbuf[pl.ds(first, 8), :, 0:128] = f0[rows, :].astype(BF16).reshape(8, SLOTS, 128)
+            wbuf[pl.ds(first, 8), :, 128:256] = f1[rows, :].astype(BF16).reshape(8, SLOTS, 128)
+            four = fr[pl.ds(pl.multiple_of(32 * i, 32), 32), :]
+            rbuf[pl.ds(first, 8)] = four.reshape(8, 4, 128).astype(BF16)
             return 0
 
-        lax.fori_loop(0, 4, turn_rest, 0)
-
-        def pack(i, _):
-            n = 128 * h + 8 * i
-            rows = pl.ds(pl.multiple_of(128 * i, 128), 128)
-            wbuf[pl.ds(n, 8), :, 0:128] = f0[rows, :].astype(BF16).reshape(8, SLOTS, 128)
-            wbuf[pl.ds(n, 8), :, 128:256] = f1[rows, :].astype(BF16).reshape(8, SLOTS, 128)
-            four = fr[pl.ds(pl.multiple_of(32 * i, 32), 32), :]
-            for m in range(8):
-                rbuf[n + m] = four[4 * m : 4 * m + 4, :].astype(BF16)
-            return 0
-
-        lax.fori_loop(0, 16, pack, 0)
+        lax.fori_loop(0, 16, pack, 0, unroll=4)
 
     def send(lat_off, lon_off):
         ta, tb = flip(a, lat_off), along(b, lon_off)
@@ -137,7 +133,7 @@
         send(0, lon_off)
         return 0
 
-    prepare(a // 8, True)
+    prepare(0)
     pl.semaphore_wait(bar, 2 * (SIDE - 1))
 
     def ready(i, _):
@@ -155,7 +151,7 @@
     lax.fori_loop(1, SIDE, send_columns, 0)
     lax.fori_loop(1, SIDE, send_lon, 0)
     lax.fori_loop(1, 8, send_lat, 0)
-    prepare(1 - a // 8, False)
+    prepare(1)
     lax.fori_loop(8, SIDE, send_lat, 0)
     own = [
         pltpu.make_async_copy(wbuf.at[me], recv.at[0], rsem.at[0, 0]),
@@ -165,12 +161,15 @@
         copy.start()
 
     def pair_of(t):
-        return jnp.where(t < 6, t + 2, 7 - t)
+        near = 2 * (3 - (t - 1) // 2) + (t - 1) % 2
+        return jnp.where(t == 0, 1, jnp.where(t == 7, 0, near))
 
     def send_pair(t):
         first = 2 * pair_of(t)
 
-        def both(lat_off, _):
+        def both(i, _):
+            lat_off = SIDE - i
+
             @pl.when(first > 0)
             def _():
                 send(lat_off, first)
@@ -221,9 +220,15 @@
     loads[4].wait()
     loads[5].wait()
 
+    def clear(r, _):
+        cur[r] = jnp.zeros((64, WIDE), F32)
+        nxt[r] = jnp.zeros((64, WIDE), F32)
+        return 0
+
+    lax.fori_loop(0, CLAT + 2, clear, 0)
+
     def begin(r, _):
         cur[r + 1, 8:56, 0:CHAN] = adj_v[r]
-        cur[r + 1, 8:56, CHAN:WIDE] = jnp.zeros((CLON, WIDE - CHAN), F32)
         return 0
 
     lax.fori_loop(0, CLAT, begin, 0)
@@ -291,17 +296,18 @@
         coef_rim[k, 0:CLAT, :] = coef[k, :, 0, :]
         coef_rim[k, CLAT : 2 * CLAT, :] = coef[k, :, CLON - 1, :]
 
-    def last_turns(t, _):
-        first = 2 * pair_of(t)
-        absorb(first)
-        absorb(first + 1)
-        return 0
-
-    lax.fori_loop(8 - LAG, 8, last_turns, 0)
+    absorb(0)
+    last = 2 * pair_of(6)
+
+    def last_turns(g, _):
+        absorb(jnp.where(g == 2, 1, last + g))
+        return 0
+
+    lax.fori_loop(0, 3, last_turns, 0)
 
     def halo(buf, e):
-        north = copy_to(buf.at[CLAT, 8:56, :], buf.at[0, 8:56, :], hs_sem.at[e, 0], hr_sem.at[e, 0], (a + 1) % SIDE, b)
-        south = copy_to(buf.at[1, 8:56, :], buf.at[CLAT + 1, 8:56, :], hs_sem.at[e, 1], hr_sem.at[e, 1], (a + SIDE - 1) % SIDE, b)
+        north = copy_to(buf.at[CLAT, 8:56, :], row_in.at[e, 0], hs_sem.at[e, 0], hr_sem.at[e, 0], (a + 1) % SIDE, b)
+        south = copy_to(buf.at[1, 8:56, :], row_in.at[e, 1], hs_sem.at[e, 1], hr_sem.at[e, 1], (a + SIDE - 1) % SIDE, b)
         east = copy_to(col_out.at[e, 0], col_in.at[e, 0], hs_sem.at[e, 2], hr_sem.at[e, 2], a, (b + 1) % SIDE)
         west = copy_to(col_out.at[e, 1], col_in.at[e, 1], hs_sem.at[e, 3], hr_sem.at[e, 3], a, (b + SIDE - 1) % SIDE)
 
@@ -326,7 +332,7 @@
 
         @pl.when(a == 0)
         def _():
-            buf[0, 8:56, :] = buf[1, 8:56, :]
+            row_in[e, 0] = buf[1, 8:56, :]
 
         @pl.when(a < SIDE - 1)
         def _():
@@ -334,7 +340,7 @@
 
         @pl.when(a == SIDE - 1)
         def _():
-            buf[CLAT + 1, 8:56, :] = buf[CLAT, 8:56, :]
+            row_in[e, 1] = buf[CLAT, 8:56, :]
 
         east.wait_recv()
         west.wait_recv()
@@ -373,26 +379,28 @@
             mh[k * CLON : (k + 1) * CLON, :], ml[k * CLON : (k + 1) * CLON, :] = split(m)
         return mixed(mh[...], ml[...], width)
 
-    def outer(buf, e, width):
-        west = col_in[e, 0, :, 0:CHAN]
-        east = col_in[e, 1, :, 0:CHAN]
-        for n, (x, x_west, x_east) in enumerate(((8, west, None), (55, None, east))):
+    def rim_inside(buf):
+        for n, x in enumerate((8, 55)):
             span = slice(n * CLAT, (n + 1) * CLAT)
-            x_west = buf[1 : CLAT + 1, x - 1, 0:CHAN] if x_west is None else x_west
-            x_east = buf[1 : CLAT + 1, x + 1, 0:CHAN] if x_east is None else x_east
             rim[span, :] = blend(
                 [coef_rim[k, span, :] for k in range(5)],
-                [buf[1 : CLAT + 1, x, 0:CHAN], x_east, x_west, buf[2 : CLAT + 2, x, 0:CHAN], buf[0:CLAT, x, 0:CHAN]],
+                [buf[1 : CLAT + 1, x, 0:CHAN], buf[1 : CLAT + 1, x + 1, 0:CHAN], buf[1 : CLAT + 1, x - 1, 0:CHAN],
+                 buf[2 : CLAT + 2, x, 0:CHAN], buf[0:CLAT, x, 0:CHAN]],
             )
         for n, r in enumerate((0, CLAT - 1)):
-            buf[r + 1, 7:8, 0:CHAN] = west[r : r + 1, :]
-            buf[r + 1, 56:57, 0:CHAN] = east[r : r + 1, :]
-            m = blend(
+            rim[2 * CLAT + n * CLON : 2 * CLAT + (n + 1) * CLON, :] = blend(
                 [coef[k, r] for k in range(5)],
                 [buf[r + 1, 8:56, 0:CHAN], buf[r + 1, 9:57, 0:CHAN], buf[r + 1, 7:55, 0:CHAN],
                  buf[r + 2, 8:56, 0:CHAN], buf[r, 8:56, 0:CHAN]],
             )
-            rim[2 * CLAT + n * CLON : 2 * CLAT + (n + 1) * CLON, :] = m
+
+    def rim_beyond(e, width):
+        rim[0:CLAT, :] += coef_rim[2, 0:CLAT, :] * col_in[e, 0, :, 0:CHAN]
+        rim[CLAT : 2 * CLAT, :] += coef_rim[1, CLAT : 2 * CLAT, :] * col_in[e, 1, :, 0:CHAN]
+        for n, r, k in ((0, 0, 4), (1, CLAT - 1, 3)):
+            rim[2 * CLAT + n * CLON : 2 * CLAT + (n + 1) * CLON, :] += coef[k, r] * row_in[e, n, :, 0:CHAN]
+            for i, x in ((r, 0), (CLAT + r, CLON - 1)):
+                rim[i : i + 1, :] += coef_rim[k, i : i + 1, :] * row_in[e, n, x : x + 1, 0:CHAN]
         return mixed(*split(rim[...]), width)
 
     col_out[0, 0, :, 0:CHAN] = cur[1 : CLAT + 1, 55, 0:CHAN]
@@ -405,12 +413,13 @@
         return 0
 
     lax.fori_loop(0, 2, inner_one, 0)
+    rim_inside(cur)
     arrive(cur, 0, one)
-    res = outer(cur, 0, CHAN)
+    res = rim_beyond(0, CHAN)
+    nxt[1, 8:56, 0:CHAN] = res[2 * CLAT : 2 * CLAT + CLON]
+    nxt[CLAT, 8:56, 0:CHAN] = res[2 * CLAT + CLON : RIM]
     nxt[1 : CLAT + 1, 8, 0:CHAN] = res[0:CLAT]
     nxt[1 : CLAT + 1, 55, 0:CHAN] = res[CLAT : 2 * CLAT]
-    nxt[1, 8:56, 0:CHAN] = res[2 * CLAT : 2 * CLAT + CLON]
-    nxt[CLAT, 8:56, 0:CHAN] = res[2 * CLAT + CLON : RIM]
     col_out[1, 0, :, 0:CHAN] = res[CLAT : 2 * CLAT]
     col_out[1, 1, :, 0:CHAN] = res[0:CLAT]
     two = halo(nxt, 1)
@@ -422,13 +431,14 @@
         return 0
 
     lax.fori_loop(0, 2, inner_two, 0)
+    rim_inside(nxt)
     arrive(nxt, 1, two)
-    res = outer(nxt, 1, WIDE)
-    for dst, lanes in ((out_v, slice(0, CHAN)), (sens, slice(256, WIDE))):
+    res = rim_beyond(1, WIDE)
+    for dst, lanes in ((sens, slice(256, WIDE)), (out_v, slice(0, CHAN))):
+        dst[0] = res[2 * CLAT : 2 * CLAT + CLON, lanes]
+        dst[CLAT - 1] = res[2 * CLAT + CLON : RIM, lanes]
         dst[:, 0, :] = res[0:CLAT, lanes]
         dst[:, CLON - 1, :] = res[CLAT : 2 * CLAT, lanes]
-        dst[0] = res[2 * CLAT : 2 * CLAT + CLON, lanes]
-        dst[CLAT - 1] = res[2 * CLAT + CLON : RIM, lanes]
     leave = pltpu.make_async_copy(out_v, out, out_sem.at[0])
     leave.start()
 
@@ -476,6 +486,22 @@
     for n, buf in enumerate((recv, recr)):
         piece = buf.at[pl.ds(1, DEVICES - 1)]
         pltpu.make_async_copy(piece, piece, ssem.at[n]).wait()
+
+
+def deliver_kernel(state, grad, state_out, grad_out, held, sems):
+    parts = 4
+    rows = CLAT // parts
+    spans = [pl.ds(i * rows, rows) for i in range(parts)]
+    reads = [pltpu.make_async_copy(state.at[p], held.at[p], sems.at[0, i]) for i, p in enumerate(spans)]
+    writes = [pltpu.make_async_copy(held.at[p], state_out.at[p], sems.at[1, i]) for i, p in enumerate(spans)]
+    for read in reads:
+        read.start()
+    grad_out[...] = grad[...].reshape(1, 1, TRACERS)
+    for read, write in zip(reads, writes):
+        read.wait()
+        write.start()
+    for write in writes:
+        write.wait()
 
 
 def body(
@@ -492,7 +518,7 @@
         in_specs=[anywhere, anywhere, vmem, vmem, anywhere, vmem, vmem, anywhere, vmem],
         out_specs=(anywhere, vmem),
         scratch_shapes=[
-            pltpu.VMEM((SLOTS, CHAN, DEVICES), BF16),
+            pltpu.VMEM((2, SLOTS, CHAN, 128), BF16),
             pltpu.VMEM((128 * SLOTS, 128), F32),
             pltpu.VMEM((128 * SLOTS, 128), F32),
             pltpu.VMEM((128 * 4, 128), F32),
@@ -520,6 +546,7 @@
             pltpu.VMEM((CLAT + 2, 64, WIDE), F32),
             pltpu.VMEM((2, 2, CLAT, WIDE), F32),
             pltpu.VMEM((2, 2, CLAT, WIDE), F32),
+            pltpu.VMEM((2, 2, CLON, WIDE), F32),
             pltpu.VMEM((ROWS * CLON, CHAN), BF16),
             pltpu.VMEM((ROWS * CLON, CHAN), BF16),
             pltpu.VMEM((RIM, CHAN), F32),
@@ -556,7 +583,18 @@
         basis.reshape(CELLS, DEVICES),
         owner.reshape(1, DEVICES),
     )
-    return state, grad.reshape(1, 1, TRACERS)
+    return pl.pallas_call(
+        deliver_kernel,
+        out_shape=(
+            jax.ShapeDtypeStruct((CLAT, CLON, CHAN), F32),
+            jax.ShapeDtypeStruct((1, 1, TRACERS), F32),
+        ),
+        in_specs=[anywhere, vmem],
+        out_specs=(anywhere, vmem),
+        scratch_shapes=[pltpu.VMEM((CLAT, CLON, CHAN), F32), pltpu.SemaphoreType.DMA((2, 4))],
+        compiler_params=pltpu.CompilerParams(vmem_limit_bytes=56 << 20),
+        name="deliver",
+    )(state, grad)
 
 
 def solution(mesh):

time: 97.9 us -> 94.4 us (0.964)
  local copies, waits for them, and re-layouts: 3.31 us -> 0 us
    pallas_call x1, Pallas kernels: 93.7 us -> 90.1 us  [body(): pl.pallas_call(window_kernel, out_shape=(jax.ShapeDtypeStruct((CLAT, CLON...]
    pallas_call x0 -> x1, Pallas kernels: none -> 3.43 us  [body(): pl.pallas_call(deliver_kernel, out_shape=(jax.ShapeDtypeStruct((CLAT, CLO...]
    unnamed x4 -> x0, local copies, waits for them, and re-layouts: 3.31 us -> none
where the time goes in v4:
time: 94.4 us; the launch traced here: 94.2 us
  Pallas kernels  93.5 us (99%)
    pallas_call x1, Pallas kernels, body(): pl.pallas_call(window_kernel, out_shape=(jax.ShapeDtypeStruct((CLAT, CLON...  90.1 us
    pallas_call x1, Pallas kernels, body(): pl.pallas_call(deliver_kernel, out_shape=(jax.ShapeDtypeStruct((CLAT, CLO...  3.43 us

profile of v4, /device:TPU:1, one launch (start us, length us, event | category | flops | bytes accessed | tf_op | source)
XLA Modules:
  0.0 94.2 jit_solution(479848355380036634)
XLA Ops:
  0.6 90.1 %window.1 = (f32[24,48,288]{2,1,0:T(8,128)}, f32[1,4]{1,0:T(1,128)}) custom-call(f32[24,48,288]{2,1,0:T(8,128)} %adj.1, f32[24,48,144]{2,1,0:T(8,128)} %winds.1, f32[72,72]{1,0:T(8,128)} %mix.1, f32[288]{0:T(512)} %lweights.1, bf16[16,288,256]{2,1,0:T(8,128)(2,1)} %bitcast.9, s32[16,256]{1,0:T(8,128)} %bitcast.11, s32[1,256]{1,0:T(1,128)} %bitcast.12, ...), custom_call_target="tpu_custom_call" | custom-call | tf_op jit(solution)/shard_map/window/pallas_call | solution.py:512
  90.8 3.4 %deliver.1 = (f32[24,48,288]{2,1,0:T(8,128)}, f32[1,1,4]{2,1,0:T(1,128)}) custom-call(f32[24,48,288]{2,1,0:T(8,128)} %get-tuple-element.4.state, f32[1,4]{1,0:T(1,128)} %get-tuple-element.5.grad), custom_call_target="tpu_custom_call" | custom-call | tf_op jit(solution)/shard_map/deliver/pallas_call | solution.py:586

commit v5 on v4

--- a/solution.py
+++ b/solution.py
@@ -53,8 +53,9 @@
     out, grad,
     w_v, f0, f1, fr, wbuf, rbuf, kbuf, kin, kmid, recv, recr, reck, stage, rhs,
     adj_v, winds_v, coef, coef_rim, basis_v, base_hi, base_lo, mat, mat_hi, mat_lo,
-    cur, nxt, col_out, col_in, row_in, mh, ml, rim, out_v, sens, gsend, gin, grow, gfin,
-    pair_sem, ssem, rsem, lsem, ks_sem, kr_sem, hs_sem, hr_sem, gs_sem, gr_sem, out_sem,
+    cur, nxt, col_out, col_in, row_in, mh, ml, rim, ring, ring_coef, ring_hi, ring_lo, out_v, sens, gsend, gin, grow, gfin,
+    winds_col, basis_col, near_winds_col, near_basis_col, near_winds_row, near_basis_row,
+    pair_sem, ns_sem, nr_sem, ssem, rsem, lsem, ks_sem, kr_sem, hs_sem, hr_sem, gs_sem, gr_sem, out_sem,
 ):
     a = lax.axis_index("lat")
     b = lax.axis_index("lon")
@@ -212,13 +213,49 @@
 
     loads[6].wait()
     pick = jnp.where(iota((DEVICES, DEVICES), 0) == owner[...], 1.0, 0.0).astype(BF16)
-    for c in range(CELLS // 128):
-        for piece, dst in zip(split(basis_v[128 * c : 128 * c + 128, :]), (base_hi, base_lo)):
-            turned = lax.dot_general(pick, piece, (((1,), (1,)), ((), ())), preferred_element_type=F32)
-            dst[:, 128 * c : 128 * c + 128] = turned.astype(BF16)
+
+    def by_owner(piece):
+        turned = lax.dot_general(pick, piece, (((1,), (1,)), ((), ())), preferred_element_type=F32)
+        return turned.astype(BF16)
+
+    for c in range(CLAT // BAND):
+        high, low = split(basis_v[BAND * c : BAND * c + BAND].reshape(BAND * CLON, DEVICES))
+        base_hi[:, BAND * CLON * c : BAND * CLON * (c + 1)] = by_owner(high)
+        base_lo[:, BAND * CLON * c : BAND * CLON * (c + 1)] = by_owner(low)
 
     loads[4].wait()
     loads[5].wait()
+
+    for n, x in enumerate((CLON - 1, 0)):
+        winds_col[n] = winds_v[:, x, 0:LEV]
+        basis_col[n] = basis_v[:, x, :]
+    lon_near = []
+    lat_near = []
+    for n, (r, tb, ta) in enumerate((
+        (CLAT - 1, (b + 1) % SIDE, (a + 1) % SIDE),
+        (0, (b + SIDE - 1) % SIDE, (a + SIDE - 1) % SIDE),
+    )):
+        for k, (col, row, col_in_, row_in_) in enumerate((
+            (winds_col, winds_v, near_winds_col, near_winds_row),
+            (basis_col, basis_v, near_basis_col, near_basis_row),
+        )):
+            lon_near.append(copy_to(col.at[n], col_in_.at[n], ns_sem.at[k, n], nr_sem.at[k, n], a, tb))
+            lat_near.append((n, copy_to(row.at[r], row_in_.at[n], ns_sem.at[k, 2 + n], nr_sem.at[k, 2 + n], ta, b)))
+    for copy in lon_near:
+        copy.start()
+    first_band, last_band = a == 0, a == SIDE - 1
+    for n, copy in lat_near:
+        @pl.when(jnp.logical_not(last_band if n == 0 else first_band))
+        def _():
+            copy.start()
+
+    for n, none in ((0, first_band), (1, last_band)):
+        @pl.when(none)
+        def _():
+            near_winds_row[n] = jnp.zeros((CLON, 2 * LEV), F32)
+            near_basis_row[n] = jnp.zeros((CLON, DEVICES), F32)
+            row_in[0, n] = jnp.zeros((CLON, WIDE), F32)
+            row_in[1, n] = jnp.zeros((CLON, WIDE), F32)
 
     def clear(r, _):
         cur[r] = jnp.zeros((64, WIDE), F32)
@@ -296,6 +333,25 @@
         coef_rim[k, 0:CLAT, :] = coef[k, :, 0, :]
         coef_rim[k, CLAT : 2 * CLAT, :] = coef[k, :, CLON - 1, :]
 
+    for copy in lon_near:
+        copy.wait_recv()
+    for n, copy in lat_near:
+        @pl.when(jnp.logical_not(first_band if n == 0 else last_band))
+        def _():
+            copy.wait_recv()
+
+    def inflow(wind):
+        return jnp.concatenate([jnp.maximum(wind, 0.0) + diffusion] * TRACERS, axis=1)
+
+    ring_coef[0:CLAT, :] = inflow(near_winds_col[0])
+    ring_coef[CLAT : 2 * CLAT, :] = inflow(-near_winds_col[1])
+    ring_coef[2 * CLAT : 2 * CLAT + CLON, :] = inflow(near_winds_row[0][:, LEV : 2 * LEV])
+    ring_coef[2 * CLAT + CLON : RIM, :] = inflow(-near_winds_row[1][:, LEV : 2 * LEV])
+    ring_basis = jnp.concatenate([near_basis_col[0], near_basis_col[1], near_basis_row[0], near_basis_row[1]], axis=0)
+    high, low = split(ring_basis)
+    ring_hi[...] = by_owner(high)
+    ring_lo[...] = by_owner(low)
+
     absorb(0)
     last = 2 * pair_of(6)
 
@@ -323,24 +379,16 @@
         west.start()
         return north, south, east, west
 
-    def arrive(buf, e, copies):
+    def arrive(copies):
         north, south, east, west = copies
 
         @pl.when(a > 0)
         def _():
             north.wait_recv()
 
-        @pl.when(a == 0)
-        def _():
-            row_in[e, 0] = buf[1, 8:56, :]
-
         @pl.when(a < SIDE - 1)
         def _():
             south.wait_recv()
-
-        @pl.when(a == SIDE - 1)
-        def _():
-            row_in[e, 1] = buf[CLAT, 8:56, :]
 
         east.wait_recv()
         west.wait_recv()
@@ -365,8 +413,8 @@
             m = m + weights[k] * values[k]
         return m
 
-    def mixed(high, low, width):
-        return dot(high, mat_hi[:, 0:width]) + dot(low, mat_hi[:, 0:width]) + dot(high, mat_lo[:, 0:width])
+    def mixed(high, low, to, start=0):
+        return dot(high, mat_hi[:, start:to]) + dot(low, mat_hi[:, start:to]) + dot(high, mat_lo[:, start:to])
 
     def inner(buf, c, width):
         for k in range(ROWS):
@@ -394,6 +442,14 @@
                  buf[r + 2, 8:56, 0:CHAN], buf[r, 8:56, 0:CHAN]],
             )
 
+        for r, k, edge in ((0, 4, first_band), (CLAT - 1, 3, last_band)):
+            @pl.when(edge)
+            def _():
+                n = min(r, 1)
+                rim[2 * CLAT + n * CLON : 2 * CLAT + (n + 1) * CLON, :] += coef[k, r] * buf[r + 1, 8:56, 0:CHAN]
+                for i, x in ((r, 8), (CLAT + r, 55)):
+                    rim[i : i + 1, :] += coef_rim[k, i : i + 1, :] * buf[r + 1, x : x + 1, 0:CHAN]
+
     def rim_beyond(e, width):
         rim[0:CLAT, :] += coef_rim[2, 0:CLAT, :] * col_in[e, 0, :, 0:CHAN]
         rim[CLAT : 2 * CLAT, :] += coef_rim[1, CLAT : 2 * CLAT, :] * col_in[e, 1, :, 0:CHAN]
@@ -414,7 +470,7 @@
 
     lax.fori_loop(0, 2, inner_one, 0)
     rim_inside(cur)
-    arrive(cur, 0, one)
+    arrive(one)
     res = rim_beyond(0, CHAN)
     nxt[1, 8:56, 0:CHAN] = res[2 * CLAT : 2 * CLAT + CLON]
     nxt[CLAT, 8:56, 0:CHAN] = res[2 * CLAT + CLON : RIM]
@@ -432,18 +488,18 @@
 
     lax.fori_loop(0, 2, inner_two, 0)
     rim_inside(nxt)
-    arrive(nxt, 1, two)
-    res = rim_beyond(1, WIDE)
-    for dst, lanes in ((sens, slice(256, WIDE)), (out_v, slice(0, CHAN))):
-        dst[0] = res[2 * CLAT : 2 * CLAT + CLON, lanes]
-        dst[CLAT - 1] = res[2 * CLAT + CLON : RIM, lanes]
-        dst[:, 0, :] = res[0:CLAT, lanes]
-        dst[:, CLON - 1, :] = res[CLAT : 2 * CLAT, lanes]
-    leave = pltpu.make_async_copy(out_v, out, out_sem.at[0])
-    leave.start()
+    ring[0:CLAT, :] = ring_coef[0:CLAT, :] * nxt[1 : CLAT + 1, 8, 0:CHAN]
+    ring[CLAT : 2 * CLAT, :] = ring_coef[CLAT : 2 * CLAT, :] * nxt[1 : CLAT + 1, 55, 0:CHAN]
+    ring[2 * CLAT : 2 * CLAT + CLON, :] = ring_coef[2 * CLAT : 2 * CLAT + CLON, :] * nxt[1, 8:56, 0:CHAN]
+    ring[2 * CLAT + CLON : RIM, :] = ring_coef[2 * CLAT + CLON : RIM, :] * nxt[CLAT, 8:56, 0:CHAN]
+    ends = mixed(*split(rim[2 * CLAT : RIM, :]), WIDE, 256)
+    sens[0] = ends[0:CLON]
+    sens[CLAT - 1] = ends[CLON : 2 * CLON]
+    beyond_hi, beyond_lo = split(mixed(*split(ring[...]), WIDE, 256))
 
     sens_hi, sens_lo = split(sens[...].reshape(CELLS, 128))
     part = dot(base_hi[...], sens_hi) + dot(base_lo[...], sens_hi) + dot(base_hi[...], sens_lo)
+    part = part + (dot(ring_hi[...], beyond_hi) + dot(ring_lo[...], beyond_hi) + dot(ring_hi[...], beyond_lo))
     rows = iota((DEVICES, 128), 0)
     lanes = iota((DEVICES, 128), 1)
     part = jnp.where((lanes // TRACERS == rows % SIDE + 8) & (lanes >= 32), part, 0.0)
@@ -455,6 +511,14 @@
         return 0
 
     lax.fori_loop(1, SIDE, give_lat, 0)
+    arrive(two)
+    res = rim_beyond(1, CHAN)
+    out_v[0] = res[2 * CLAT : 2 * CLAT + CLON]
+    out_v[CLAT - 1] = res[2 * CLAT + CLON : RIM]
+    out_v[:, 0, :] = res[0:CLAT]
+    out_v[:, CLON - 1, :] = res[CLAT : 2 * CLAT]
+    leave = pltpu.make_async_copy(out_v, out, out_sem.at[0])
+    leave.start()
     got = gsend[a]
     lat_in = gin.at[pl.ds(1, SIDE - 1)]
     pltpu.make_async_copy(lat_in, lat_in, gr_sem.at[0]).wait()
@@ -476,10 +540,18 @@
     for t in range(TRACERS):
         value = jnp.sum(jnp.where(lanes == 32 + TRACERS * b + t, got, 0.0), axis=1, keepdims=True)
         owned = jnp.where(iota((1, TRACERS), 1) == t, value, owned)
-    grad[...] = owned * (1.0 / jnp.sqrt(jnp.full((1, TRACERS), CELLS * DEVICES, F32)))
+    owned = owned * (1.0 / jnp.sqrt(jnp.full((1, TRACERS), CELLS * DEVICES, F32)))
+    grad[...] = owned.reshape(1, 1, TRACERS)
 
     finish(one)
     finish(two)
+    for copy in lon_near:
+        copy.wait_send()
+    for n, copy in lat_near:
+        @pl.when(jnp.logical_not(last_band if n == 0 else first_band))
+        def _():
+            copy.wait_send()
+
     leave.wait()
     for piece, sem in ((landed, ks_sem.at[0]), (coming, ks_sem.at[1]), (lat_in, gs_sem.at[0]), (lon_in, gs_sem.at[1])):
         pltpu.make_async_copy(piece, piece, sem).wait()
@@ -488,15 +560,17 @@
         pltpu.make_async_copy(piece, piece, ssem.at[n]).wait()
 
 
-def deliver_kernel(state, grad, state_out, grad_out, held, sems):
+def deliver_kernel(state, grad, state_out, grad_out, held, small, sems):
     parts = 4
     rows = CLAT // parts
-    spans = [pl.ds(i * rows, rows) for i in range(parts)]
-    reads = [pltpu.make_async_copy(state.at[p], held.at[p], sems.at[0, i]) for i, p in enumerate(spans)]
-    writes = [pltpu.make_async_copy(held.at[p], state_out.at[p], sems.at[1, i]) for i, p in enumerate(spans)]
+    reads = [pltpu.make_async_copy(grad, small, sems.at[0, parts])]
+    writes = [pltpu.make_async_copy(small, grad_out, sems.at[1, parts])]
+    for i in range(parts):
+        span = pl.ds(i * rows, rows)
+        reads.append(pltpu.make_async_copy(state.at[span], held.at[span], sems.at[0, i]))
+        writes.append(pltpu.make_async_copy(held.at[span], state_out.at[span], sems.at[1, i]))
     for read in reads:
         read.start()
-    grad_out[...] = grad[...].reshape(1, 1, TRACERS)
     for read, write in zip(reads, writes):
         read.wait()
         write.start()
@@ -513,7 +587,7 @@
         window_kernel,
         out_shape=(
             jax.ShapeDtypeStruct((CLAT, CLON, CHAN), F32),
-            jax.ShapeDtypeStruct((1, TRACERS), F32),
+            jax.ShapeDtypeStruct((1, 1, TRACERS), F32),
         ),
         in_specs=[anywhere, anywhere, vmem, vmem, anywhere, vmem, vmem, anywhere, vmem],
         out_specs=(anywhere, vmem),
@@ -536,7 +610,7 @@
             pltpu.VMEM((CLAT, CLON, 2 * LEV), F32),
             pltpu.VMEM((5, CLAT, CLON, CHAN), F32),
             pltpu.VMEM((5, 2 * CLAT, CHAN), F32),
-            pltpu.VMEM((CELLS, DEVICES), F32),
+            pltpu.VMEM((CLAT, CLON, DEVICES), F32),
             pltpu.VMEM((DEVICES, CELLS), BF16),
             pltpu.VMEM((DEVICES, CELLS), BF16),
             pltpu.VMEM((CHAN, WIDE), F32),
@@ -550,13 +624,25 @@
             pltpu.VMEM((ROWS * CLON, CHAN), BF16),
             pltpu.VMEM((ROWS * CLON, CHAN), BF16),
             pltpu.VMEM((RIM, CHAN), F32),
+            pltpu.VMEM((RIM, CHAN), F32),
+            pltpu.VMEM((RIM, CHAN), F32),
+            pltpu.VMEM((DEVICES, RIM), BF16),
+            pltpu.VMEM((DEVICES, RIM), BF16),
             pltpu.VMEM((CLAT, CLON, CHAN), F32),
             pltpu.VMEM((CLAT, CLON, 128), F32),
             pltpu.VMEM((SIDE, 1, 128), F32),
             pltpu.VMEM((SIDE, 1, 128), F32),
             pltpu.VMEM((1, 128), F32),
             pltpu.VMEM((SIDE, 1, 128), F32),
+            pltpu.VMEM((2, CLAT, LEV), F32),
+            pltpu.VMEM((2, CLAT, DEVICES), F32),
+            pltpu.VMEM((2, CLAT, LEV), F32),
+            pltpu.VMEM((2, CLAT, DEVICES), F32),
+            pltpu.VMEM((2, CLON, 2 * LEV), F32),
+            pltpu.VMEM((2, CLON, DEVICES), F32),
             pltpu.SemaphoreType.REGULAR,
+            pltpu.SemaphoreType.DMA((2, 4)),
+            pltpu.SemaphoreType.DMA((2, 4)),
             pltpu.SemaphoreType.DMA((2,)),
             pltpu.SemaphoreType.DMA((2, SIDE)),
             pltpu.SemaphoreType.DMA((7,)),
@@ -580,7 +666,7 @@
         jnp.transpose(snd_weights[0, 0], (1, 2, 0)),
         jnp.transpose(snd_columns[0, 0], (1, 0)),
         snd_counts[0],
-        basis.reshape(CELLS, DEVICES),
+        basis,
         owner.reshape(1, DEVICES),
     )
     return pl.pallas_call(
@@ -589,9 +675,13 @@
             jax.ShapeDtypeStruct((CLAT, CLON, CHAN), F32),
             jax.ShapeDtypeStruct((1, 1, TRACERS), F32),
         ),
-        in_specs=[anywhere, vmem],
-        out_specs=(anywhere, vmem),
-        scratch_shapes=[pltpu.VMEM((CLAT, CLON, CHAN), F32), pltpu.SemaphoreType.DMA((2, 4))],
+        in_specs=[anywhere, anywhere],
+        out_specs=(anywhere, anywhere),
+        scratch_shapes=[
+            pltpu.VMEM((CLAT, CLON, CHAN), F32),
+            pltpu.VMEM((1, 1, TRACERS), F32),
+            pltpu.SemaphoreType.DMA((2, 5)),
+        ],
         compiler_params=pltpu.CompilerParams(vmem_limit_bytes=56 << 20),
         name="deliver",
     )(state, grad)

time: 94.4 us -> 92.8 us (0.983)
  Pallas kernels: 93.5 us -> 91.9 us
    pallas_call x1, Pallas kernels: 3.43 us -> 2.3 us  [body(): pl.pallas_call(deliver_kernel, out_shape=(jax.ShapeDtypeStruct((CLAT, CLO...]
where the time goes in v5:
time: 92.8 us; the launch traced here: 92.6 us
  Pallas kernels  91.9 us (99%)
    pallas_call x1, Pallas kernels, body(): pl.pallas_call(window_kernel, out_shape=(jax.ShapeDtypeStruct((CLAT, CLON...  89.6 us
    pallas_call x1, Pallas kernels, body(): pl.pallas_call(deliver_kernel, out_shape=(jax.ShapeDtypeStruct((CLAT, CLO...  2.3 us

profile of v5, /device:TPU:1, one launch (start us, length us, event | category | flops | bytes accessed | tf_op | source)
XLA Modules:
  0.0 92.6 jit_solution(2444189519796931664)
XLA Ops:
  0.6 89.6 %window.1 = (f32[24,48,288]{2,1,0:T(8,128)}, f32[1,1,4]{2,1,0:T(1,128)}) custom-call(f32[24,48,288]{2,1,0:T(8,128)} %adj.1, f32[24,48,144]{2,1,0:T(8,128)} %winds.1, f32[72,72]{1,0:T(8,128)} %mix.1, f32[288]{0:T(512)} %lweights.1, bf16[16,288,256]{2,1,0:T(8,128)(2,1)} %bitcast.8, s32[16,256]{1,0:T(8,128)} %bitcast.9, s32[1,256]{1,0:T(1,128)} %bitcast.10, ...), custom_call_target="tpu_custom_call" | custom-call | tf_op jit(solution)/shard_map/window/pallas_call | solution.py:586
  90.3 2.3 %deliver.1 = (f32[24,48,288]{2,1,0:T(8,128)}, f32[1,1,4]{2,1,0:T(1,128)}) custom-call(f32[24,48,288]{2,1,0:T(8,128)} %get-tuple-element.4.state, f32[1,1,4]{2,1,0:T(1,128)} %get-tuple-element.5.grad), custom_call_target="tpu_custom_call" | custom-call | tf_op jit(solution)/shard_map/deliver/pallas_call | solution.py:672

commit v6 on v5

--- a/solution.py
+++ b/solution.py
@@ -52,8 +52,8 @@
     adj, winds, mix, lweights, w, columns, counts, basis, owner,
     out, grad,
     w_v, f0, f1, fr, wbuf, rbuf, kbuf, kin, kmid, recv, recr, reck, stage, rhs,
-    adj_v, winds_v, coef, coef_rim, basis_v, base_hi, base_lo, mat, mat_hi, mat_lo,
-    cur, nxt, col_out, col_in, row_in, mh, ml, rim, ring, ring_coef, ring_hi, ring_lo, out_v, sens, gsend, gin, grow, gfin,
+    adj_v, winds_v, coef, coef_rim, basis_v, base_hi, base_lo, mat, mat_hi, mat_lo, mat_end,
+    cur, nxt, col_out, col_in, row_in, mh, ml, rim, ring_coef, ring_hi, ring_lo, out_v, sens, gsend, gin, grow, gfin,
     winds_col, basis_col, near_winds_col, near_basis_col, near_winds_row, near_basis_row,
     pair_sem, ns_sem, nr_sem, ssem, rsem, lsem, ks_sem, kr_sem, hs_sem, hr_sem, gs_sem, gr_sem, out_sem,
 ):
@@ -209,7 +209,8 @@
     lane = iota((CHAN, WIDE - CHAN), 1)
     extra = (iota((CHAN, WIDE - CHAN), 0) // LEV == lane % TRACERS) & (lane < TRACERS * SIDE)
     mat[:, CHAN:WIDE] = jnp.where(extra, gain, 0.0)
-    mat_hi[...], mat_lo[...] = split(mat[...])
+    mat_hi[...], mat_lo[...] = split(mat[:, 0:256])
+    mat_end[:, 0:128], mat_end[:, 128:256] = split(mat[:, 256:WIDE])
 
     loads[6].wait()
     pick = jnp.where(iota((DEVICES, DEVICES), 0) == owner[...], 1.0, 0.0).astype(BF16)
@@ -413,10 +414,17 @@
             m = m + weights[k] * values[k]
         return m
 
-    def mixed(high, low, to, start=0):
-        return dot(high, mat_hi[:, start:to]) + dot(low, mat_hi[:, start:to]) + dot(high, mat_lo[:, start:to])
-
-    def inner(buf, c, width):
+    def mixed(high, low):
+        return dot(high, mat_hi[...]) + dot(low, mat_hi[...]) + dot(high, mat_lo[...])
+
+    def mixed_end(high, low, start=0):
+        both = dot(high[:, start:], mat_end[start:, :])
+        return both[:, 0:128] + both[:, 128:256] + dot(low[:, start:], mat_end[start:, 0:128])
+
+    def span_of(c):
+        return pl.ds(pl.multiple_of(c * ROWS * CLON, 16), ROWS * CLON)
+
+    def inner(buf, c):
         for k in range(ROWS):
             r = 1 + c * ROWS + k
             m = blend(
@@ -424,8 +432,9 @@
                 [buf[r + 1, 8:56, 0:CHAN], buf[r + 1, 9:57, 0:CHAN], buf[r + 1, 7:55, 0:CHAN],
                  buf[r + 2, 8:56, 0:CHAN], buf[r, 8:56, 0:CHAN]],
             )
-            mh[k * CLON : (k + 1) * CLON, :], ml[k * CLON : (k + 1) * CLON, :] = split(m)
-        return mixed(mh[...], ml[...], width)
+            rows = pl.ds(pl.multiple_of((c * ROWS + k) * CLON, 16), CLON)
+            mh[rows, :], ml[rows, :] = split(m)
+        return mh[span_of(c), :], ml[span_of(c), :]
 
     def rim_inside(buf):
         for n, x in enumerate((8, 55)):
@@ -450,56 +459,62 @@
                 for i, x in ((r, 8), (CLAT + r, 55)):
                     rim[i : i + 1, :] += coef_rim[k, i : i + 1, :] * buf[r + 1, x : x + 1, 0:CHAN]
 
-    def rim_beyond(e, width):
+    def rim_beyond(e):
         rim[0:CLAT, :] += coef_rim[2, 0:CLAT, :] * col_in[e, 0, :, 0:CHAN]
         rim[CLAT : 2 * CLAT, :] += coef_rim[1, CLAT : 2 * CLAT, :] * col_in[e, 1, :, 0:CHAN]
         for n, r, k in ((0, 0, 4), (1, CLAT - 1, 3)):
             rim[2 * CLAT + n * CLON : 2 * CLAT + (n + 1) * CLON, :] += coef[k, r] * row_in[e, n, :, 0:CHAN]
             for i, x in ((r, 0), (CLAT + r, CLON - 1)):
                 rim[i : i + 1, :] += coef_rim[k, i : i + 1, :] * row_in[e, n, x : x + 1, 0:CHAN]
-        return mixed(*split(rim[...]), width)
+        parts = split(rim[0:RIM, :])
+        return (slice(0, 256), mixed(*parts)), (slice(256, CHAN), mixed_end(*parts, 128)[:, 0 : CHAN - 256])
 
     col_out[0, 0, :, 0:CHAN] = cur[1 : CLAT + 1, 55, 0:CHAN]
     col_out[0, 1, :, 0:CHAN] = cur[1 : CLAT + 1, 8, 0:CHAN]
     one = halo(cur, 0)
 
     def inner_one(c, _):
-        res = inner(cur, c, CHAN).reshape(ROWS, CLON, CHAN)
-        nxt[pl.ds(c * ROWS + 2, ROWS), 8:56, 0:CHAN] = res
+        high, low = inner(cur, c)
+        rows = pl.ds(c * ROWS + 2, ROWS)
+        nxt[rows, 8:56, 0:256] = mixed(high, low).reshape(ROWS, CLON, 256)
+        end = mixed_end(high, low, 128)[:, 0 : CHAN - 256]
+        nxt[rows, 8:56, 256:CHAN] = end.reshape(ROWS, CLON, CHAN - 256)
         return 0
 
     lax.fori_loop(0, 2, inner_one, 0)
     rim_inside(cur)
     arrive(one)
-    res = rim_beyond(0, CHAN)
-    nxt[1, 8:56, 0:CHAN] = res[2 * CLAT : 2 * CLAT + CLON]
-    nxt[CLAT, 8:56, 0:CHAN] = res[2 * CLAT + CLON : RIM]
-    nxt[1 : CLAT + 1, 8, 0:CHAN] = res[0:CLAT]
-    nxt[1 : CLAT + 1, 55, 0:CHAN] = res[CLAT : 2 * CLAT]
-    col_out[1, 0, :, 0:CHAN] = res[CLAT : 2 * CLAT]
-    col_out[1, 1, :, 0:CHAN] = res[0:CLAT]
+    for lanes, res in rim_beyond(0):
+        nxt[1, 8:56, lanes] = res[2 * CLAT : 2 * CLAT + CLON]
+        nxt[CLAT, 8:56, lanes] = res[2 * CLAT + CLON : RIM]
+        nxt[1 : CLAT + 1, 8, lanes] = res[0:CLAT]
+        nxt[1 : CLAT + 1, 55, lanes] = res[CLAT : 2 * CLAT]
+        col_out[1, 0, :, lanes] = res[CLAT : 2 * CLAT]
+        col_out[1, 1, :, lanes] = res[0:CLAT]
     two = halo(nxt, 1)
 
-    def inner_two(c, _):
-        res = inner(nxt, c, WIDE)
-        out_v[pl.ds(c * ROWS + 1, ROWS)] = res[:, 0:CHAN].reshape(ROWS, CLON, CHAN)
-        sens[pl.ds(c * ROWS + 1, ROWS)] = res[:, 256:WIDE].reshape(ROWS, CLON, 128)
-        return 0
-
-    lax.fori_loop(0, 2, inner_two, 0)
+    def inner_sens(c, _):
+        end = mixed_end(*inner(nxt, c)).reshape(ROWS, CLON, 128)
+        sens[pl.ds(c * ROWS + 1, ROWS)] = end
+        out_v[pl.ds(c * ROWS + 1, ROWS), :, 256:CHAN] = end[:, :, 0 : CHAN - 256]
+        return 0
+
+    lax.fori_loop(0, 2, inner_sens, 0)
+
     rim_inside(nxt)
-    ring[0:CLAT, :] = ring_coef[0:CLAT, :] * nxt[1 : CLAT + 1, 8, 0:CHAN]
-    ring[CLAT : 2 * CLAT, :] = ring_coef[CLAT : 2 * CLAT, :] * nxt[1 : CLAT + 1, 55, 0:CHAN]
-    ring[2 * CLAT : 2 * CLAT + CLON, :] = ring_coef[2 * CLAT : 2 * CLAT + CLON, :] * nxt[1, 8:56, 0:CHAN]
-    ring[2 * CLAT + CLON : RIM, :] = ring_coef[2 * CLAT + CLON : RIM, :] * nxt[CLAT, 8:56, 0:CHAN]
-    ends = mixed(*split(rim[2 * CLAT : RIM, :]), WIDE, 256)
+    rim[RIM : RIM + CLAT, :] = ring_coef[0:CLAT, :] * nxt[1 : CLAT + 1, 8, 0:CHAN]
+    rim[RIM + CLAT : RIM + 2 * CLAT, :] = ring_coef[CLAT : 2 * CLAT, :] * nxt[1 : CLAT + 1, 55, 0:CHAN]
+    rim[RIM + 2 * CLAT : RIM + 2 * CLAT + CLON, :] = ring_coef[2 * CLAT : 2 * CLAT + CLON, :] * nxt[1, 8:56, 0:CHAN]
+    rim[RIM + 2 * CLAT + CLON : 2 * RIM, :] = ring_coef[2 * CLAT + CLON : RIM, :] * nxt[CLAT, 8:56, 0:CHAN]
+    ends = mixed_end(*split(rim[2 * CLAT : 2 * RIM, :]))
     sens[0] = ends[0:CLON]
     sens[CLAT - 1] = ends[CLON : 2 * CLON]
-    beyond_hi, beyond_lo = split(mixed(*split(ring[...]), WIDE, 256))
+    beyond_hi, beyond_lo = split(ends[2 * CLON :])
 
     sens_hi, sens_lo = split(sens[...].reshape(CELLS, 128))
-    part = dot(base_hi[...], sens_hi) + dot(base_lo[...], sens_hi) + dot(base_hi[...], sens_lo)
-    part = part + (dot(ring_hi[...], beyond_hi) + dot(ring_lo[...], beyond_hi) + dot(ring_hi[...], beyond_lo))
+    both = dot(base_hi[...], jnp.concatenate([sens_hi, sens_lo], axis=1))
+    both = both + dot(ring_hi[...], jnp.concatenate([beyond_hi, beyond_lo], axis=1))
+    part = both[:, 0:128] + both[:, 128:256] + (dot(base_lo[...], sens_hi) + dot(ring_lo[...], beyond_hi))
     rows = iota((DEVICES, 128), 0)
     lanes = iota((DEVICES, 128), 1)
     part = jnp.where((lanes // TRACERS == rows % SIDE + 8) & (lanes >= 32), part, 0.0)
@@ -511,12 +526,19 @@
         return 0
 
     lax.fori_loop(1, SIDE, give_lat, 0)
+
+    def inner_state(c, _):
+        res = mixed(mh[span_of(c), :], ml[span_of(c), :])
+        out_v[pl.ds(c * ROWS + 1, ROWS), :, 0:256] = res.reshape(ROWS, CLON, 256)
+        return 0
+
+    lax.fori_loop(0, 2, inner_state, 0)
     arrive(two)
-    res = rim_beyond(1, CHAN)
-    out_v[0] = res[2 * CLAT : 2 * CLAT + CLON]
-    out_v[CLAT - 1] = res[2 * CLAT + CLON : RIM]
-    out_v[:, 0, :] = res[0:CLAT]
-    out_v[:, CLON - 1, :] = res[CLAT : 2 * CLAT]
+    for lanes, res in rim_beyond(1):
+        out_v[0, :, lanes] = res[2 * CLAT : 2 * CLAT + CLON]
+        out_v[CLAT - 1, :, lanes] = res[2 * CLAT + CLON : RIM]
+        out_v[:, 0, lanes] = res[0:CLAT]
+        out_v[:, CLON - 1, lanes] = res[CLAT : 2 * CLAT]
     leave = pltpu.make_async_copy(out_v, out, out_sem.at[0])
     leave.start()
     got = gsend[a]
@@ -614,17 +636,17 @@
             pltpu.VMEM((DEVICES, CELLS), BF16),
             pltpu.VMEM((DEVICES, CELLS), BF16),
             pltpu.VMEM((CHAN, WIDE), F32),
-            pltpu.VMEM((CHAN, WIDE), BF16),
-            pltpu.VMEM((CHAN, WIDE), BF16),
+            pltpu.VMEM((CHAN, 256), BF16),
+            pltpu.VMEM((CHAN, 256), BF16),
+            pltpu.VMEM((CHAN, 256), BF16),
             pltpu.VMEM((CLAT + 2, 64, WIDE), F32),
             pltpu.VMEM((CLAT + 2, 64, WIDE), F32),
             pltpu.VMEM((2, 2, CLAT, WIDE), F32),
             pltpu.VMEM((2, 2, CLAT, WIDE), F32),
             pltpu.VMEM((2, 2, CLON, WIDE), F32),
-            pltpu.VMEM((ROWS * CLON, CHAN), BF16),
-            pltpu.VMEM((ROWS * CLON, CHAN), BF16),
-            pltpu.VMEM((RIM, CHAN), F32),
-            pltpu.VMEM((RIM, CHAN), F32),
+            pltpu.VMEM((2 * ROWS * CLON, CHAN), BF16),
+            pltpu.VMEM((2 * ROWS * CLON, CHAN), BF16),
+            pltpu.VMEM((2 * RIM, CHAN), F32),
             pltpu.VMEM((RIM, CHAN), F32),
             pltpu.VMEM((DEVICES, RIM), BF16),
             pltpu.VMEM((DEVICES, RIM), BF16),

time: 92.8 us -> 92.2 us (level)
  no operation moved by 1% of the time
where the time goes in v6:
time: 92.2 us; the launch traced here: 92 us
  Pallas kernels  91.4 us (99%)
    pallas_call x1, Pallas kernels, body(): pl.pallas_call(window_kernel, out_shape=(jax.ShapeDtypeStruct((CLAT, CLON...  89.1 us
    pallas_call x1, Pallas kernels, body(): pl.pallas_call(deliver_kernel, out_shape=(jax.ShapeDtypeStruct((CLAT, CLO...  2.3 us

profile of v6, /device:TPU:1, one launch (start us, length us, event | category | flops | bytes accessed | tf_op | source)
XLA Modules:
  0.0 92.0 jit_solution(17148201704138906196)
XLA Ops:
  0.6 89.1 %window.1 = (f32[24,48,288]{2,1,0:T(8,128)}, f32[1,1,4]{2,1,0:T(1,128)}) custom-call(f32[24,48,288]{2,1,0:T(8,128)} %adj.1, f32[24,48,144]{2,1,0:T(8,128)} %winds.1, f32[72,72]{1,0:T(8,128)} %mix.1, f32[288]{0:T(512)} %lweights.1, bf16[16,288,256]{2,1,0:T(8,128)(2,1)} %bitcast.8, s32[16,256]{1,0:T(8,128)} %bitcast.9, s32[1,256]{1,0:T(1,128)} %bitcast.10, ...), custom_call_target="tpu_custom_call" | custom-call | tf_op jit(solution)/shard_map/window/pallas_call | solution.py:608
  89.7 2.3 %deliver.1 = (f32[24,48,288]{2,1,0:T(8,128)}, f32[1,1,4]{2,1,0:T(1,128)}) custom-call(f32[24,48,288]{2,1,0:T(8,128)} %get-tuple-element.4.state, f32[1,1,4]{2,1,0:T(1,128)} %get-tuple-element.5.grad), custom_call_target="tpu_custom_call" | custom-call | tf_op jit(solution)/shard_map/deliver/pallas_call | solution.py:694

commit v7 on v6

--- a/solution.py
+++ b/solution.py
@@ -24,6 +24,10 @@
 RIM = 2 * CLAT + 2 * CLON
 
 
+FAR_LAT = (10, 6, 11, 9, 7, 5, 8, 14, 2, 13, 3, 12, 4, 15, 1)
+FAR_LON = (4, 12, 3, 5, 11, 13, 2, 6, 10, 14, 1, 7, 9, 15, 8)
+
+
 def flip(index, by):
     return sum(((index // k) % 2 + (by // k) % 2) % 2 * k for k in (8, 4, 2, 1))
 
@@ -62,11 +66,6 @@
     me = a * SIDE + b
     bar = pltpu.get_barrier_semaphore()
 
-    def greet(i, _):
-        pl.semaphore_signal(bar, inc=1, device_id=((a + i) % SIDE, b), device_id_type=MESH)
-        pl.semaphore_signal(bar, inc=1, device_id=(a, (b + i) % SIDE), device_id_type=MESH)
-        return 0
-
     halves = [a // 8, 1 - a // 8]
     loads = []
     for n, h in enumerate(halves):
@@ -76,7 +75,9 @@
             loads.append(pltpu.make_async_copy(w.at[eight, :, lanes], w_v.at[n, eight], lsem.at[2 * n + q]))
     for load in loads:
         load.start()
-    lax.fori_loop(1, SIDE, greet, 0)
+    for i, j in zip(FAR_LAT, FAR_LON):
+        pl.semaphore_signal(bar, inc=1, device_id=(a, (b + j) % SIDE), device_id_type=MESH)
+        pl.semaphore_signal(bar, inc=1, device_id=((a + i) % SIDE, b), device_id_type=MESH)
     loads.append(pltpu.make_async_copy(adj, adj_v, lsem.at[4]))
     loads.append(pltpu.make_async_copy(winds, winds_v, lsem.at[5]))
     loads.append(pltpu.make_async_copy(basis, basis_v, lsem.at[6]))
@@ -130,18 +131,15 @@
         send(lat_off, 0)
         return 0
 
-    def send_lon(lon_off, _):
-        send(0, lon_off)
+    def send_lon(i, _):
+        send(0, jnp.where(i <= 2, i + 1, jnp.where(i == SIDE - 1, 1, 18 - i)))
         return 0
 
     prepare(0)
     pl.semaphore_wait(bar, 2 * (SIDE - 1))
 
-    def ready(i, _):
-        pl.semaphore_signal(pair_sem, inc=1, device_id=(a, (b + i) % SIDE), device_id_type=MESH)
-        return 0
-
-    lax.fori_loop(1, SIDE, ready, 0)
+    for j in FAR_LON:
+        pl.semaphore_signal(pair_sem, inc=1, device_id=(a, (b + j) % SIDE), device_id_type=MESH)
 
     def send_columns(lat_off, _):
         ta = flip(a, lat_off)
@@ -149,8 +147,8 @@
         copy_to(src, kin.at[lat_off], ks_sem.at[0], kr_sem.at[0], ta, b).start()
         return 0
 
+    lax.fori_loop(1, SIDE, send_lon, 0)
     lax.fori_loop(1, SIDE, send_columns, 0)
-    lax.fori_loop(1, SIDE, send_lon, 0)
     lax.fori_loop(1, 8, send_lat, 0)
     prepare(1)
     lax.fori_loop(8, SIDE, send_lat, 0)
@@ -520,12 +518,9 @@
     part = jnp.where((lanes // TRACERS == rows % SIDE + 8) & (lanes >= 32), part, 0.0)
     gsend[:, 0, :] = jnp.sum(part.reshape(SIDE, SIDE, 128), axis=1)
 
-    def give_lat(i, _):
+    for i in FAR_LAT:
         ta = (a + i) % SIDE
         copy_to(gsend.at[ta], gin.at[i], gs_sem.at[0], gr_sem.at[0], ta, b).start()
-        return 0
-
-    lax.fori_loop(1, SIDE, give_lat, 0)
 
     def inner_state(c, _):
         res = mixed(mh[span_of(c), :], ml[span_of(c), :])
@@ -548,11 +543,8 @@
         got = got + gin[i]
     grow[...] = got
 
-    def give_lon(i, _):
-        copy_to(grow, gfin.at[i], gs_sem.at[1], gr_sem.at[1], a, (b + i) % SIDE).start()
-        return 0
-
-    lax.fori_loop(1, SIDE, give_lon, 0)
+    for j in FAR_LON:
+        copy_to(grow, gfin.at[j], gs_sem.at[1], gr_sem.at[1], a, (b + j) % SIDE).start()
     lon_in = gfin.at[pl.ds(1, SIDE - 1)]
     pltpu.make_async_copy(lon_in, lon_in, gr_sem.at[1]).wait()
     for i in range(1, SIDE):

time: 92.2 us -> 91.8 us (level)
  no operation moved by 1% of the time
where the time goes in v7:
time: 91.8 us; the launch traced here: 91.6 us
  Pallas kernels  91 us (99%)
    pallas_call x1, Pallas kernels, body(): pl.pallas_call(window_kernel, out_shape=(jax.ShapeDtypeStruct((CLAT, CLON...  88.7 us
    pallas_call x1, Pallas kernels, body(): pl.pallas_call(deliver_kernel, out_shape=(jax.ShapeDtypeStruct((CLAT, CLO...  2.3 us

profile of v7, /device:TPU:1, one launch (start us, length us, event | category | flops | bytes accessed | tf_op | source)
XLA Modules:
  0.0 91.6 jit_solution(466186401366592126)
XLA Ops:
  0.6 88.7 %window.1 = (f32[24,48,288]{2,1,0:T(8,128)}, f32[1,1,4]{2,1,0:T(1,128)}) custom-call(f32[24,48,288]{2,1,0:T(8,128)} %adj.1, f32[24,48,144]{2,1,0:T(8,128)} %winds.1, f32[72,72]{1,0:T(8,128)} %mix.1, f32[288]{0:T(512)} %lweights.1, bf16[16,288,256]{2,1,0:T(8,128)(2,1)} %bitcast.8, s32[16,256]{1,0:T(8,128)} %bitcast.9, s32[1,256]{1,0:T(1,128)} %bitcast.10, ...), custom_call_target="tpu_custom_call" | custom-call | tf_op jit(solution)/shard_map/window/pallas_call | solution.py:600
  89.3 2.3 %deliver.1 = (f32[24,48,288]{2,1,0:T(8,128)}, f32[1,1,4]{2,1,0:T(1,128)}) custom-call(f32[24,48,288]{2,1,0:T(8,128)} %get-tuple-element.4.state, f32[1,1,4]{2,1,0:T(1,128)} %get-tuple-element.5.grad), custom_call_target="tpu_custom_call" | custom-call | tf_op jit(solution)/shard_map/deliver/pallas_call | solution.py:686

commit v8 on v7

--- a/solution.py
+++ b/solution.py
@@ -79,8 +79,8 @@
         pl.semaphore_signal(bar, inc=1, device_id=(a, (b + j) % SIDE), device_id_type=MESH)
         pl.semaphore_signal(bar, inc=1, device_id=((a + i) % SIDE, b), device_id_type=MESH)
     loads.append(pltpu.make_async_copy(adj, adj_v, lsem.at[4]))
-    loads.append(pltpu.make_async_copy(winds, winds_v, lsem.at[5]))
-    loads.append(pltpu.make_async_copy(basis, basis_v, lsem.at[6]))
+    loads.append(pltpu.make_async_copy(winds, winds_v.at[pl.ds(0, CLAT)], lsem.at[5]))
+    loads.append(pltpu.make_async_copy(basis, basis_v.at[pl.ds(0, CLAT)], lsem.at[6]))
     for load in loads[4:]:
         load.start()
 
@@ -226,8 +226,8 @@
     loads[5].wait()
 
     for n, x in enumerate((CLON - 1, 0)):
-        winds_col[n] = winds_v[:, x, 0:LEV]
-        basis_col[n] = basis_v[:, x, :]
+        winds_col[n] = winds_v[0:CLAT, x, 0:LEV]
+        basis_col[n] = basis_v[0:CLAT, x, :]
     lon_near = []
     lat_near = []
     for n, (r, tb, ta) in enumerate((
@@ -301,7 +301,7 @@
         rhs[:, 0:256] = recv[pl.ds(first, SIDE)].reshape(256, 256)
         for m in range(SIDE):
             stage[4 * m : 4 * m + 4, :] = recr[first + m].astype(F32)
-        wide = (dot(spread, stage[...].astype(BF16)) * keep).astype(BF16)
+        wide = (dot(spread, stage[0:64, :].astype(BF16)) * keep).astype(BF16)
         rhs[:, 256:384] = dot(wide, fold).astype(BF16)
         spot = reck[g]
         for c in range(CLAT // BAND):
@@ -329,8 +329,8 @@
 
     lax.fori_loop(LAG, 8, turn, 0)
     for k in range(5):
-        coef_rim[k, 0:CLAT, :] = coef[k, :, 0, :]
-        coef_rim[k, CLAT : 2 * CLAT, :] = coef[k, :, CLON - 1, :]
+        coef_rim[k, 0:CLAT, :] = coef[k, 0:CLAT, 0, :]
+        coef_rim[k, CLAT : 2 * CLAT, :] = coef[k, 0:CLAT, CLON - 1, :]
 
     for copy in lon_near:
         copy.wait_recv()
@@ -509,7 +509,7 @@
     sens[CLAT - 1] = ends[CLON : 2 * CLON]
     beyond_hi, beyond_lo = split(ends[2 * CLON :])
 
-    sens_hi, sens_lo = split(sens[...].reshape(CELLS, 128))
+    sens_hi, sens_lo = split(sens[0:CLAT].reshape(CELLS, 128))
     both = dot(base_hi[...], jnp.concatenate([sens_hi, sens_lo], axis=1))
     both = both + dot(ring_hi[...], jnp.concatenate([beyond_hi, beyond_lo], axis=1))
     part = both[:, 0:128] + both[:, 128:256] + (dot(base_lo[...], sens_hi) + dot(ring_lo[...], beyond_hi))
@@ -532,9 +532,9 @@
     for lanes, res in rim_beyond(1):
         out_v[0, :, lanes] = res[2 * CLAT : 2 * CLAT + CLON]
         out_v[CLAT - 1, :, lanes] = res[2 * CLAT + CLON : RIM]
-        out_v[:, 0, lanes] = res[0:CLAT]
-        out_v[:, CLON - 1, lanes] = res[CLAT : 2 * CLAT]
-    leave = pltpu.make_async_copy(out_v, out, out_sem.at[0])
+        out_v[0:CLAT, 0, lanes] = res[0:CLAT]
+        out_v[0:CLAT, CLON - 1, lanes] = res[CLAT : 2 * CLAT]
+    leave = pltpu.make_async_copy(out_v.at[pl.ds(0, CLAT)], out, out_sem.at[0])
     leave.start()
     got = gsend[a]
     lat_in = gin.at[pl.ds(1, SIDE - 1)]
@@ -607,9 +607,9 @@
         out_specs=(anywhere, vmem),
         scratch_shapes=[
             pltpu.VMEM((2, SLOTS, CHAN, 128), BF16),
-            pltpu.VMEM((128 * SLOTS, 128), F32),
-            pltpu.VMEM((128 * SLOTS, 128), F32),
-            pltpu.VMEM((128 * 4, 128), F32),
+            pltpu.VMEM((129 * SLOTS, 128), F32),
+            pltpu.VMEM((129 * SLOTS, 128), F32),
+            pltpu.VMEM((130 * 4, 128), F32),
             pltpu.VMEM((DEVICES, SLOTS, 256), BF16),
             pltpu.VMEM((DEVICES, 4, 128), BF16),
             pltpu.VMEM((DEVICES, 128), jnp.int32),
@@ -618,13 +618,13 @@
             pltpu.VMEM((DEVICES, SLOTS, 256), BF16),
             pltpu.VMEM((DEVICES, 4, 128), BF16),
             pltpu.VMEM((SIDE, 1, 256), jnp.int32),
-            pltpu.VMEM((64, 128), F32),
+            pltpu.VMEM((72, 128), F32),
             pltpu.VMEM((256, WIDE), BF16),
             pltpu.VMEM((CLAT, CLON, CHAN), F32),
-            pltpu.VMEM((CLAT, CLON, 2 * LEV), F32),
-            pltpu.VMEM((5, CLAT, CLON, CHAN), F32),
+            pltpu.VMEM((CLAT + 1, CLON, 2 * LEV), F32),
+            pltpu.VMEM((5, CLAT + 1, CLON, CHAN), F32),
             pltpu.VMEM((5, 2 * CLAT, CHAN), F32),
-            pltpu.VMEM((CLAT, CLON, DEVICES), F32),
+            pltpu.VMEM((CLAT + 1, CLON, DEVICES), F32),
             pltpu.VMEM((DEVICES, CELLS), BF16),
             pltpu.VMEM((DEVICES, CELLS), BF16),
             pltpu.VMEM((CHAN, WIDE), F32),
@@ -635,15 +635,15 @@
             pltpu.VMEM((CLAT + 2, 64, WIDE), F32),
             pltpu.VMEM((2, 2, CLAT, WIDE), F32),
             pltpu.VMEM((2, 2, CLAT, WIDE), F32),
-            pltpu.VMEM((2, 2, CLON, WIDE), F32),
+            pltpu.VMEM((3, 2, CLON, WIDE), F32),
             pltpu.VMEM((2 * ROWS * CLON, CHAN), BF16),
             pltpu.VMEM((2 * ROWS * CLON, CHAN), BF16),
             pltpu.VMEM((2 * RIM, CHAN), F32),
             pltpu.VMEM((RIM, CHAN), F32),
             pltpu.VMEM((DEVICES, RIM), BF16),
             pltpu.VMEM((DEVICES, RIM), BF16),
-            pltpu.VMEM((CLAT, CLON, CHAN), F32),
-            pltpu.VMEM((CLAT, CLON, 128), F32),
+            pltpu.VMEM((CLAT + 1, CLON, CHAN), F32),
+            pltpu.VMEM((CLAT + 1, CLON, 128), F32),
             pltpu.VMEM((SIDE, 1, 128), F32),
             pltpu.VMEM((SIDE, 1, 128), F32),
             pltpu.VMEM((1, 128), F32),

time: 91.8 us -> 91.8 us (level)
  no operation moved by 1% of the time
where the time goes in v8:
time: 91.8 us; the launch traced here: 91.6 us
  Pallas kernels  91 us (99%)
    pallas_call x1, Pallas kernels, body(): pl.pallas_call(window_kernel, out_shape=(jax.ShapeDtypeStruct((CLAT, CLON...  88.7 us
    pallas_call x1, Pallas kernels, body(): pl.pallas_call(deliver_kernel, out_shape=(jax.ShapeDtypeStruct((CLAT, CLO...  2.3 us

profile of v8, /device:TPU:1, one launch (start us, length us, event | category | flops | bytes accessed | tf_op | source)
XLA Modules:
  0.0 91.6 jit_solution(14657596343040060732)
XLA Ops:
  0.6 88.7 %window.1 = (f32[24,48,288]{2,1,0:T(8,128)}, f32[1,1,4]{2,1,0:T(1,128)}) custom-call(f32[24,48,288]{2,1,0:T(8,128)} %adj.1, f32[24,48,144]{2,1,0:T(8,128)} %winds.1, f32[72,72]{1,0:T(8,128)} %mix.1, f32[288]{0:T(512)} %lweights.1, bf16[16,288,256]{2,1,0:T(8,128)(2,1)} %bitcast.8, s32[16,256]{1,0:T(8,128)} %bitcast.9, s32[1,256]{1,0:T(1,128)} %bitcast.10, ...), custom_call_target="tpu_custom_call" | custom-call | tf_op jit(solution)/shard_map/window/pallas_call | solution.py:600
  89.3 2.3 %deliver.1 = (f32[24,48,288]{2,1,0:T(8,128)}, f32[1,1,4]{2,1,0:T(1,128)}) custom-call(f32[24,48,288]{2,1,0:T(8,128)} %get-tuple-element.4.state, f32[1,1,4]{2,1,0:T(1,128)} %get-tuple-element.5.grad), custom_call_target="tpu_custom_call" | custom-call | tf_op jit(solution)/shard_map/deliver/pallas_call | solution.py:686

commit v9 on v8

--- a/solution.py
+++ b/solution.py
@@ -360,7 +360,7 @@
 
     lax.fori_loop(0, 3, last_turns, 0)
 
-    def halo(buf, e):
+    def halo(buf, e, columns):
         north = copy_to(buf.at[CLAT, 8:56, :], row_in.at[e, 0], hs_sem.at[e, 0], hr_sem.at[e, 0], (a + 1) % SIDE, b)
         south = copy_to(buf.at[1, 8:56, :], row_in.at[e, 1], hs_sem.at[e, 1], hr_sem.at[e, 1], (a + SIDE - 1) % SIDE, b)
         east = copy_to(col_out.at[e, 0], col_in.at[e, 0], hs_sem.at[e, 2], hr_sem.at[e, 2], a, (b + 1) % SIDE)
@@ -374,6 +374,7 @@
         def _():
             south.start()
 
+        columns()
         east.start()
         west.start()
         return north, south, east, west
@@ -467,9 +468,11 @@
         parts = split(rim[0:RIM, :])
         return (slice(0, 256), mixed(*parts)), (slice(256, CHAN), mixed_end(*parts, 128)[:, 0 : CHAN - 256])
 
-    col_out[0, 0, :, 0:CHAN] = cur[1 : CLAT + 1, 55, 0:CHAN]
-    col_out[0, 1, :, 0:CHAN] = cur[1 : CLAT + 1, 8, 0:CHAN]
-    one = halo(cur, 0)
+    def first_columns():
+        col_out[0, 0, :, 0:CHAN] = cur[1 : CLAT + 1, 55, 0:CHAN]
+        col_out[0, 1, :, 0:CHAN] = cur[1 : CLAT + 1, 8, 0:CHAN]
+
+    one = halo(cur, 0, first_columns)
 
     def inner_one(c, _):
         high, low = inner(cur, c)
@@ -489,7 +492,7 @@
         nxt[1 : CLAT + 1, 55, lanes] = res[CLAT : 2 * CLAT]
         col_out[1, 0, :, lanes] = res[CLAT : 2 * CLAT]
         col_out[1, 1, :, lanes] = res[0:CLAT]
-    two = halo(nxt, 1)
+    two = halo(nxt, 1, lambda: None)
 
     def inner_sens(c, _):
         end = mixed_end(*inner(nxt, c)).reshape(ROWS, CLON, 128)

time: 91.8 us -> 91.8 us (level)
  no operation moved by 1% of the time
where the time goes in v9:
time: 91.8 us; the launch traced here: 91.6 us
  Pallas kernels  90.9 us (99%)
    pallas_call x1, Pallas kernels, body(): pl.pallas_call(window_kernel, out_shape=(jax.ShapeDtypeStruct((CLAT, CLON...  88.6 us
    pallas_call x1, Pallas kernels, body(): pl.pallas_call(deliver_kernel, out_shape=(jax.ShapeDtypeStruct((CLAT, CLO...  2.3 us

profile of v9, /device:TPU:1, one launch (start us, length us, event | category | flops | bytes accessed | tf_op | source)
XLA Modules:
  0.0 91.6 jit_solution(3931486215308659257)
XLA Ops:
  0.6 88.6 %window.1 = (f32[24,48,288]{2,1,0:T(8,128)}, f32[1,1,4]{2,1,0:T(1,128)}) custom-call(f32[24,48,288]{2,1,0:T(8,128)} %adj.1, f32[24,48,144]{2,1,0:T(8,128)} %winds.1, f32[72,72]{1,0:T(8,128)} %mix.1, f32[288]{0:T(512)} %lweights.1, bf16[16,288,256]{2,1,0:T(8,128)(2,1)} %bitcast.8, s32[16,256]{1,0:T(8,128)} %bitcast.9, s32[1,256]{1,0:T(1,128)} %bitcast.10, ...), custom_call_target="tpu_custom_call" | custom-call | tf_op jit(solution)/shard_map/window/pallas_call | solution.py:603
  89.3 2.3 %deliver.1 = (f32[24,48,288]{2,1,0:T(8,128)}, f32[1,1,4]{2,1,0:T(1,128)}) custom-call(f32[24,48,288]{2,1,0:T(8,128)} %get-tuple-element.4.state, f32[1,1,4]{2,1,0:T(1,128)} %get-tuple-element.5.grad), custom_call_target="tpu_custom_call" | custom-call | tf_op jit(solution)/shard_map/deliver/pallas_call | solution.py:689
